TPU v7x, 512 devices: a whole 4x4x16 slice. The times are simulated.
512 devices in a mesh: gx: 32 (over x, z_hi, core), gy: 16 (over z_lo, y).
Axes of the slice: x: 4, y: 4, z: 16 (z_hi: 4, z_lo: 4; z = z_hi * 4 + z_lo), core: 2. Of those that a mesh axis runs over, the one named last changes fastest.
Arguments:
- coarse: bfloat16 [64, 64, 8, 256], P('gx', 'gy'), may hold values from -6 to 6
- skip: bfloat16 [128, 128, 16, 128], P('gx', 'gy'), may hold values from -6 to 6
- up_weight: bfloat16 [16384, 128], replicated, may hold values from -0.125 to 0.125
- up_bias: float32 [128], replicated, may hold values from -3 to 3
- first_weight: bfloat16 [6912, 128], replicated, may hold values from -0.078125 to 0.078125
- first_bias: float32 [128], replicated, may hold values from -3 to 3
- second_weight: bfloat16 [3456, 128], replicated, may hold values from -0.15625 to 0.15625
- second_bias: float32 [128], replicated, may hold values from -3 to 3
Outputs:
- refined: bfloat16 [128, 128, 16, 128], P('gx', 'gy')
All inputs are finite; a program needn't handle non-finite values.
Results may differ from a plain program's by a relative error of at most 0.011.
Values may be sent and summed in bfloat16 or wider, within the bound.
No kernel may reach another device: no remote copies, remote signals or barrier semaphores. Data moves between devices by JAX's collectives and lax.ppermute only.
A program may use at most 64 MiB of HBM per device.

v0:
```python
import jax
import jax.numpy as jnp
from jax import lax
from jax.sharding import PartitionSpec as P


def with_halo(value, sides, width):
    for axis, dim in sides:
        size, length = (lax.axis_size(axis), value.shape[dim])
        up = [(i, (i + 1) % size) for i in range(size - 1)]
        down = [(j, i) for i, j in up]
        last = lax.slice_in_dim(value, length - width, length, axis=dim)
        leading = lax.slice_in_dim(value, 0, width, axis=dim)
        before = lax.ppermute(last, axis, up)
        after = lax.ppermute(leading, axis, down)
        value = jnp.concatenate([before, value, after], axis=dim)
    return value


def fold_axis(terms, cell_axis):
    tap_axis = cell_axis + 3
    lower = lax.slice_in_dim(terms, 0, 2, axis=tap_axis)
    upper = lax.slice_in_dim(terms, 2, 4, axis=tap_axis)
    after = [(0, 0)] * terms.ndim
    before = [(0, 0)] * terms.ndim
    after[cell_axis] = (0, 1)
    before[cell_axis] = (1, 0)
    return jnp.pad(lower, after) + jnp.pad(upper, before)


def partial_upsample(coarse, weight):
    extent_x, extent_y, extent_z, in_width = coarse.shape
    out_width = weight.shape[1]
    table = (
        weight.reshape(64, in_width, out_width).transpose(1, 0, 2).reshape(in_width, 64 * out_width)
    )
    terms = jnp.dot(coarse.reshape(-1, in_width), table, preferred_element_type=jnp.float32)
    terms = terms.reshape(extent_x, extent_y, extent_z, 4, 4, 4, out_width)
    for cell_axis in range(3):
        terms = fold_axis(terms, cell_axis)
    terms = terms.transpose(0, 3, 1, 4, 2, 5, 6)
    full = terms.reshape(2 * extent_x + 2, 2 * extent_y + 2, 2 * extent_z + 2, out_width)[
        :, :, 1:-1
    ]
    ends_x = jnp.concatenate([full[0:1], full[-1:]], 0)
    got_x = with_halo(ends_x.astype(jnp.bfloat16), (("gx", 0),), 1).astype(ends_x.dtype)
    inner = full[1:-1]
    inner = inner.at[0].add(got_x[0]).at[-1].add(got_x[3])
    ends_y = jnp.concatenate([inner[:, 0:1], inner[:, -1:]], 1)
    got_y = with_halo(ends_y.astype(jnp.bfloat16), (("gy", 1),), 1).astype(ends_y.dtype)
    inner = inner[:, 1:-1]
    inner = inner.at[:, 0].add(got_y[:, 0]).at[:, -1].add(got_y[:, 3])
    return inner


def conv_block(padded, weight, extent_x, extent_y, extent_z):
    in_width = padded.shape[3]
    out_width = weight.shape[1]
    kernel = weight.reshape(3, 9 * in_width, out_width)
    total = jnp.zeros((extent_x * extent_y * extent_z, out_width), jnp.float32)
    for step_x in range(3):
        slices = []
        for step_y in range(3):
            for step_z in range(3):
                window = padded[
                    step_x : step_x + extent_x,
                    step_y : step_y + extent_y,
                    step_z : step_z + extent_z,
                ]
                slices.append(window.reshape(-1, in_width))
        total = total + jnp.dot(
            jnp.concatenate(slices, 1), kernel[step_x], preferred_element_type=jnp.float32
        )
    return total.reshape(extent_x, extent_y, extent_z, out_width)


def pad_depth(field):
    return jnp.pad(field, ((0, 0), (0, 0), (1, 1), (0, 0)))


def per_device(
    coarse, skip, up_weight, up_bias, first_weight, first_bias, second_weight, second_bias
):
    fine_x, fine_y, fine_z = (skip.shape[0], skip.shape[1], skip.shape[2])
    summed = partial_upsample(coarse, up_weight)
    upsampled = (summed + up_bias).astype(jnp.bfloat16)
    joined = jnp.concatenate([upsampled, skip], -1)
    padded = with_halo(joined, (("gx", 0), ("gy", 1)), 1)
    hidden = jnp.maximum(
        conv_block(pad_depth(padded), first_weight, fine_x, fine_y, fine_z) + first_bias, 0.0
    ).astype(jnp.bfloat16)
    hidden_grown = with_halo(hidden, (("gx", 0), ("gy", 1)), 1)
    refined = (
        conv_block(pad_depth(hidden_grown), second_weight, fine_x, fine_y, fine_z) + second_bias
    )
    return refined.astype(jnp.bfloat16)


def solution(mesh):
    return jax.shard_map(
        per_device,
        mesh=mesh,
        in_specs=(
            P("gx", "gy", None, None),
            P("gx", "gy", None, None),
            P(),
            P(),
            P(),
            P(),
            P(),
            P(),
        ),
        out_specs=P("gx", "gy", None, None),
        check_vma=False,
    )
```

profile of v0, /device:TPU:38, one launch (start us, length us, event | category | flops | bytes accessed | tf_op | source)
XLA Modules:
  0.0 102.2 jit_solution(13608575936768303434)
XLA Ops:
  0.0 6.4 %copy.10 = bf16[256,64,128]{0,2,1:T(8,128)(2,1)} copy(bf16[256,64,128]{2,0,1:T(8,128)(2,1)} %bitcast.81) | data formatting | bytes 8388608 | tf_op jit(solution)/shard_map/transpose | solution.py:35
  6.4 3.6 %fusion.31 = f32[2,4,8,4,4,4,128]{6,2,5,4,3,1,0:T(8,128)S(1)} fusion(bf16[4,4,4,128,256,1,1]{4,3,2,1,0,6,5:T(8,128)(2,1)} %bitcast.82, bf16[2,4,8,256]{3,2,1,0:T(8,128)(2,1)S(1)} %copy-done), kind=kOutput, calls=%fused_computation.133 | convolution fusion | flops 268435456 | bytes 6324224 | tf_op jit(solution)/shard_map/dot_general | solution.py:37
  11.5 11.7 %collective-permute-start.1 = (bf16[1,10,16,128]{3,2,1,0:T(8,128)(2,1)S(1)}, bf16[1,10,16,128]{3,2,1,0:T(8,128)(2,1)S(1)}, u32[]{:S(2)}, u32[]{:S(2)}) collective-permute-start(bf16[1,10,16,128]{3,2,1,0:T(8,128)(2,1)S(1)} %get-tuple-element.106), channel_id=1, source_target_pairs={{16,0},{32,16},{48,32},{64,48},{80,64},{96,80},{112,96},{128,112},... | collective-permute-start | bytes 122888 | tf_op jit(solution)/shard_map/ppermute | solution.py:15
  23.2 1.9 %collective-permute-start = (bf16[1,10,16,128]{3,2,1,0:T(8,128)(2,1)S(1)}, bf16[1,10,16,128]{3,2,1,0:T(8,128)(2,1)S(1)}, u32[]{:S(2)}, u32[]{:S(2)}) collective-permute-start(bf16[1,10,16,128]{3,2,1,0:T(8,128)(2,1)S(1)} %get-tuple-element.105), channel_id=1, source_target_pairs={{0,16},{16,32},{32,48},{48,64},{64,80},{80,96},{96,112},{112,128},... | collective-permute-start | bytes 122888 | tf_op jit(solution)/shard_map/ppermute | solution.py:14
  25.2 8.2 %collective-permute-done = bf16[1,10,16,128]{3,2,1,0:T(8,128)(2,1)S(1)} collective-permute-done((bf16[1,10,16,128]{3,2,1,0:T(8,128)(2,1)S(1)}, bf16[1,10,16,128]{3,2,1,0:T(8,128)(2,1)S(1)}, u32[]{:S(2)}, u32[]{:S(2)}) %collective-permute-start) | collective-permute-done | bytes 40992 | tf_op jit(solution)/shard_map/ppermute | solution.py:14
  33.4 5.4 %collective-permute-start.3 = (bf16[4,1,16,128]{3,2,1,0:T(8,128)(2,1)S(1)}, bf16[4,1,16,128]{3,2,1,0:T(8,128)(2,1)S(1)}, u32[]{:S(2)}, u32[]{:S(2)}) collective-permute-start(bf16[4,1,16,128]{3,2,1,0:T(8,128)(2,1)S(1)} %get-tuple-element.123), channel_id=1, source_target_pairs={{1,0},{2,1},{3,2},{4,3},{5,4},{6,5},{7,6},{8,7},{9,8},{10,9},{11,1... | collective-permute-start | bytes 49160 | tf_op jit(solution)/shard_map/ppermute | solution.py:15
  38.8 1.9 %collective-permute-start.2 = (bf16[4,1,16,128]{3,2,1,0:T(8,128)(2,1)S(1)}, bf16[4,1,16,128]{3,2,1,0:T(8,128)(2,1)S(1)}, u32[]{:S(2)}, u32[]{:S(2)}) collective-permute-start(bf16[4,1,16,128]{3,2,1,0:T(8,128)(2,1)S(1)} %get-tuple-element.122), channel_id=1, source_target_pairs={{0,1},{1,2},{2,3},{3,4},{4,5},{5,6},{6,7},{7,8},{8,9},{9,10},{10,1... | collective-permute-start | bytes 49160 | tf_op jit(solution)/shard_map/ppermute | solution.py:14
  40.8 5.8 %collective-permute-done.2 = bf16[4,1,16,128]{3,2,1,0:T(8,128)(2,1)S(1)} collective-permute-done((bf16[4,1,16,128]{3,2,1,0:T(8,128)(2,1)S(1)}, bf16[4,1,16,128]{3,2,1,0:T(8,128)(2,1)S(1)}, u32[]{:S(2)}, u32[]{:S(2)}) %collective-permute-start.2) | collective-permute-done | bytes 16416 | tf_op jit(solution)/shard_map/ppermute | solution.py:14
  46.7 1.9 %collective-permute-start.5 = (bf16[1,8,16,256]{3,2,1,0:T(8,128)(2,1)S(1)}, bf16[1,8,16,256]{3,2,1,0:T(8,128)(2,1)S(1)}, u32[]{:S(2)}, u32[]{:S(2)}) collective-permute-start(bf16[1,8,16,256]{3,2,1,0:T(8,128)(2,1)S(1)} %get-tuple-element.111), channel_id=1, source_target_pairs={{16,0},{32,16},{48,32},{64,48},{80,64},{96,80},{112,96},{128,112},... | collective-permute-start | bytes 196616 | tf_op jit(solution)/shard_map/ppermute | solution.py:15
  48.6 2.4 %collective-permute-start.4 = (bf16[1,8,16,256]{3,2,1,0:T(8,128)(2,1)S(1)}, bf16[1,8,16,256]{3,2,1,0:T(8,128)(2,1)S(1)}, u32[]{:S(2)}, u32[]{:S(2)}) collective-permute-start(bf16[1,8,16,256]{3,2,1,0:T(8,128)(2,1)S(1)} %get-tuple-element.110), channel_id=1, source_target_pairs={{0,16},{16,32},{32,48},{48,64},{64,80},{80,96},{96,112},{112,128},... | collective-permute-start | bytes 196616 | tf_op jit(solution)/shard_map/ppermute | solution.py:14
  51.0 8.8 %collective-permute-done.4 = bf16[1,8,16,256]{3,2,1,0:T(8,128)(2,1)S(1)} collective-permute-done((bf16[1,8,16,256]{3,2,1,0:T(8,128)(2,1)S(1)}, bf16[1,8,16,256]{3,2,1,0:T(8,128)(2,1)S(1)}, u32[]{:S(2)}, u32[]{:S(2)}) %collective-permute-start.4) | collective-permute-done | bytes 65568 | tf_op jit(solution)/shard_map/ppermute | solution.py:14
  59.8 1.9 %collective-permute-start.7 = (bf16[6,1,16,256]{3,2,1,0:T(8,128)(2,1)S(1)}, bf16[6,1,16,256]{3,2,1,0:T(8,128)(2,1)S(1)}, u32[]{:S(2)}, u32[]{:S(2)}) collective-permute-start(bf16[6,1,16,256]{3,2,1,0:T(8,128)(2,1)S(1)} %get-tuple-element.86), channel_id=1, source_target_pairs={{1,0},{2,1},{3,2},{4,3},{5,4},{6,5},{7,6},{8,7},{9,8},{10,9},{11,1... | collective-permute-start | bytes 147464 | tf_op jit(solution)/shard_map/ppermute | solution.py:15
  61.7 3.9 %collective-permute-start.6 = (bf16[6,1,16,256]{3,2,1,0:T(8,128)(2,1)S(1)}, bf16[6,1,16,256]{3,2,1,0:T(8,128)(2,1)S(1)}, u32[]{:S(2)}, u32[]{:S(2)}) collective-permute-start(bf16[6,1,16,256]{3,2,1,0:T(8,128)(2,1)S(1)} %get-tuple-element.85), channel_id=1, source_target_pairs={{0,1},{1,2},{2,3},{3,4},{4,5},{5,6},{6,7},{7,8},{8,9},{9,10},{10,1... | collective-permute-start | bytes 147464 | tf_op jit(solution)/shard_map/ppermute | solution.py:14
  65.8 4.0 %collective-permute-done.6 = bf16[6,1,16,256]{3,2,1,0:T(8,128)(2,1)S(1)} collective-permute-done((bf16[6,1,16,256]{3,2,1,0:T(8,128)(2,1)S(1)}, bf16[6,1,16,256]{3,2,1,0:T(8,128)(2,1)S(1)}, u32[]{:S(2)}, u32[]{:S(2)}) %collective-permute-start.6) | collective-permute-done | bytes 49184 | tf_op jit(solution)/shard_map/ppermute | solution.py:14
  69.8 0.4 select_maximum_fusion
  70.3 0.7 fusion.34
  71.5 1.3 %copy-done.3 = bf16[6912,128]{1,0:T(8,128)(2,1)S(1)} copy-done((bf16[6912,128]{1,0:T(8,128)(2,1)S(1)}, bf16[6912,128]{1,0:T(8,128)(2,1)}, u32[]{:S(2)}) %copy-start.3) | copy-done | bytes 1769496
  72.8 0.8 fusion.12
  73.8 0.8 convolution_add_fusion.3
  74.9 0.8 convolution_add_fusion.2
  75.7 1.9 %collective-permute-start.9 = (bf16[1,8,16,128]{3,2,1,0:T(8,128)(2,1)S(1)}, bf16[1,8,16,128]{3,2,1,0:T(8,128)(2,1)S(1)}, u32[]{:S(2)}, u32[]{:S(2)}) collective-permute-start(bf16[1,8,16,128]{3,2,1,0:T(8,128)(2,1)S(1)} %get-tuple-element.127), channel_id=1, source_target_pairs={{16,0},{32,16},{48,32},{64,48},{80,64},{96,80},{112,96},{128,112},... | collective-permute-start | bytes 98312 | tf_op jit(solution)/shard_map/ppermute | solution.py:15
  77.7 2.4 %collective-permute-start.8 = (bf16[1,8,16,128]{3,2,1,0:T(8,128)(2,1)S(1)}, bf16[1,8,16,128]{3,2,1,0:T(8,128)(2,1)S(1)}, u32[]{:S(2)}, u32[]{:S(2)}) collective-permute-start(bf16[1,8,16,128]{3,2,1,0:T(8,128)(2,1)S(1)} %get-tuple-element.126), channel_id=1, source_target_pairs={{0,16},{16,32},{32,48},{48,64},{64,80},{80,96},{96,112},{112,128},... | collective-permute-start | bytes 98312 | tf_op jit(solution)/shard_map/ppermute | solution.py:14
  80.1 7.6 %collective-permute-done.8 = bf16[1,8,16,128]{3,2,1,0:T(8,128)(2,1)S(1)} collective-permute-done((bf16[1,8,16,128]{3,2,1,0:T(8,128)(2,1)S(1)}, bf16[1,8,16,128]{3,2,1,0:T(8,128)(2,1)S(1)}, u32[]{:S(2)}, u32[]{:S(2)}) %collective-permute-start.8) | collective-permute-done | bytes 32800 | tf_op jit(solution)/shard_map/ppermute | solution.py:14
  87.7 1.9 %collective-permute-start.11 = (bf16[6,1,16,128]{3,2,1,0:T(8,128)(2,1)S(1)}, bf16[6,1,16,128]{3,2,1,0:T(8,128)(2,1)S(1)}, u32[]{:S(2)}, u32[]{:S(2)}) collective-permute-start(bf16[6,1,16,128]{3,2,1,0:T(8,128)(2,1)S(1)} %get-tuple-element.121), channel_id=1, source_target_pairs={{1,0},{2,1},{3,2},{4,3},{5,4},{6,5},{7,6},{8,7},{9,8},{10,9},{11,1... | collective-permute-start | bytes 73736 | tf_op jit(solution)/shard_map/ppermute | solution.py:15
  89.7 3.9 %collective-permute-start.10 = (bf16[6,1,16,128]{3,2,1,0:T(8,128)(2,1)S(1)}, bf16[6,1,16,128]{3,2,1,0:T(8,128)(2,1)S(1)}, u32[]{:S(2)}, u32[]{:S(2)}) collective-permute-start(bf16[6,1,16,128]{3,2,1,0:T(8,128)(2,1)S(1)} %get-tuple-element.120), channel_id=1, source_target_pairs={{0,1},{1,2},{2,3},{3,4},{4,5},{5,6},{6,7},{7,8},{8,9},{9,10},{10,1... | collective-permute-start | bytes 73736 | tf_op jit(solution)/shard_map/ppermute | solution.py:14
  93.6 3.9 %collective-permute-done.10 = bf16[6,1,16,128]{3,2,1,0:T(8,128)(2,1)S(1)} collective-permute-done((bf16[6,1,16,128]{3,2,1,0:T(8,128)(2,1)S(1)}, bf16[6,1,16,128]{3,2,1,0:T(8,128)(2,1)S(1)}, u32[]{:S(2)}, u32[]{:S(2)}) %collective-permute-start.10) | collective-permute-done | bytes 24608 | tf_op jit(solution)/shard_map/ppermute | solution.py:14
  97.7 0.4 fusion.37
  98.9 0.7 copy-done.2
  99.6 0.5 fusion.22
  100.2 0.5 convolution_add_fusion.1
  101.0 0.5 convolution_add_fusion
  101.5 0.7 add_convert_fusion
  (102 shorter events, 3.9 us)
Async XLA Ops:
  0.0 6.4 %copy-start = (bf16[2,4,8,256]{3,2,1,0:T(8,128)(2,1)S(1)}, bf16[2,4,8,256]{3,2,1,0:T(8,128)(2,1)}, u32[]{:S(2)}) copy-start(bf16[2,4,8,256]{3,2,1,0:T(8,128)(2,1)} %param.16) | copy-start | bytes 98308
  11.5 35.1 %copy-start.5 = (f32[128]{0:T(128)S(1)}, f32[128]{0:T(128)}, u32[]{:S(2)}) copy-start(f32[128]{0:T(128)} %param.19) | copy-start | bytes 1540
  11.5 35.1 %copy-start.1 = (bf16[4,8,16,128]{3,2,1,0:T(8,128)(2,1)S(1)}, bf16[4,8,16,128]{3,2,1,0:T(8,128)(2,1)}, u32[]{:S(2)}) copy-start(bf16[4,8,16,128]{3,2,1,0:T(8,128)(2,1)} %param.17) | copy-start | bytes 393220
  11.5 13.7 %collective-permute-start.1 = (bf16[1,10,16,128]{3,2,1,0:T(8,128)(2,1)S(1)}, bf16[1,10,16,128]{3,2,1,0:T(8,128)(2,1)S(1)}, u32[]{:S(2)}, u32[]{:S(2)}) collective-permute-start(bf16[1,10,16,128]{3,2,1,0:T(8,128)(2,1)S(1)} %get-tuple-element.106), channel_id=1, source_target_pairs={{16,0},{32,16},{48,32},{64,48},{80,64},{96,80},{112,96},{128,112},... | collective-permute-start | bytes 122888 | tf_op jit(solution)/shard_map/ppermute | solution.py:15
  23.2 10.1 %collective-permute-start = (bf16[1,10,16,128]{3,2,1,0:T(8,128)(2,1)S(1)}, bf16[1,10,16,128]{3,2,1,0:T(8,128)(2,1)S(1)}, u32[]{:S(2)}, u32[]{:S(2)}) collective-permute-start(bf16[1,10,16,128]{3,2,1,0:T(8,128)(2,1)S(1)} %get-tuple-element.105), channel_id=1, source_target_pairs={{0,16},{16,32},{32,48},{48,64},{64,80},{80,96},{96,112},{112,128},... | collective-permute-start | bytes 122888 | tf_op jit(solution)/shard_map/ppermute | solution.py:14
  33.4 7.3 %collective-permute-start.3 = (bf16[4,1,16,128]{3,2,1,0:T(8,128)(2,1)S(1)}, bf16[4,1,16,128]{3,2,1,0:T(8,128)(2,1)S(1)}, u32[]{:S(2)}, u32[]{:S(2)}) collective-permute-start(bf16[4,1,16,128]{3,2,1,0:T(8,128)(2,1)S(1)} %get-tuple-element.123), channel_id=1, source_target_pairs={{1,0},{2,1},{3,2},{4,3},{5,4},{6,5},{7,6},{8,7},{9,8},{10,9},{11,1... | collective-permute-start | bytes 49160 | tf_op jit(solution)/shard_map/ppermute | solution.py:15
  38.8 7.7 %collective-permute-start.2 = (bf16[4,1,16,128]{3,2,1,0:T(8,128)(2,1)S(1)}, bf16[4,1,16,128]{3,2,1,0:T(8,128)(2,1)S(1)}, u32[]{:S(2)}, u32[]{:S(2)}) collective-permute-start(bf16[4,1,16,128]{3,2,1,0:T(8,128)(2,1)S(1)} %get-tuple-element.122), channel_id=1, source_target_pairs={{0,1},{1,2},{2,3},{3,4},{4,5},{5,6},{6,7},{7,8},{8,9},{9,10},{10,1... | collective-permute-start | bytes 49160 | tf_op jit(solution)/shard_map/ppermute | solution.py:14
  46.7 4.3 %collective-permute-start.5 = (bf16[1,8,16,256]{3,2,1,0:T(8,128)(2,1)S(1)}, bf16[1,8,16,256]{3,2,1,0:T(8,128)(2,1)S(1)}, u32[]{:S(2)}, u32[]{:S(2)}) collective-permute-start(bf16[1,8,16,256]{3,2,1,0:T(8,128)(2,1)S(1)} %get-tuple-element.111), channel_id=1, source_target_pairs={{16,0},{32,16},{48,32},{64,48},{80,64},{96,80},{112,96},{128,112},... | collective-permute-start | bytes 196616 | tf_op jit(solution)/shard_map/ppermute | solution.py:15
  48.6 11.2 %collective-permute-start.4 = (bf16[1,8,16,256]{3,2,1,0:T(8,128)(2,1)S(1)}, bf16[1,8,16,256]{3,2,1,0:T(8,128)(2,1)S(1)}, u32[]{:S(2)}, u32[]{:S(2)}) collective-permute-start(bf16[1,8,16,256]{3,2,1,0:T(8,128)(2,1)S(1)} %get-tuple-element.110), channel_id=1, source_target_pairs={{0,16},{16,32},{32,48},{48,64},{64,80},{80,96},{96,112},{112,128},... | collective-permute-start | bytes 196616 | tf_op jit(solution)/shard_map/ppermute | solution.py:14
  59.8 6.0 %collective-permute-start.7 = (bf16[6,1,16,256]{3,2,1,0:T(8,128)(2,1)S(1)}, bf16[6,1,16,256]{3,2,1,0:T(8,128)(2,1)S(1)}, u32[]{:S(2)}, u32[]{:S(2)}) collective-permute-start(bf16[6,1,16,256]{3,2,1,0:T(8,128)(2,1)S(1)} %get-tuple-element.86), channel_id=1, source_target_pairs={{1,0},{2,1},{3,2},{4,3},{5,4},{6,5},{7,6},{8,7},{9,8},{10,9},{11,1... | collective-permute-start | bytes 147464 | tf_op jit(solution)/shard_map/ppermute | solution.py:15
  61.7 8.1 %collective-permute-start.6 = (bf16[6,1,16,256]{3,2,1,0:T(8,128)(2,1)S(1)}, bf16[6,1,16,256]{3,2,1,0:T(8,128)(2,1)S(1)}, u32[]{:S(2)}, u32[]{:S(2)}) collective-permute-start(bf16[6,1,16,256]{3,2,1,0:T(8,128)(2,1)S(1)} %get-tuple-element.85), channel_id=1, source_target_pairs={{0,1},{1,2},{2,3},{3,4},{4,5},{5,6},{6,7},{7,8},{8,9},{9,10},{10,1... | collective-permute-start | bytes 147464 | tf_op jit(solution)/shard_map/ppermute | solution.py:14
  71.4 1.5 %copy-start.3 = (bf16[6912,128]{1,0:T(8,128)(2,1)S(1)}, bf16[6912,128]{1,0:T(8,128)(2,1)}, u32[]{:S(2)}) copy-start(bf16[6912,128]{1,0:T(8,128)(2,1)} %param.20) | copy-start | bytes 5308420
  74.9 0.8 copy-start.4
  75.7 4.3 %collective-permute-start.9 = (bf16[1,8,16,128]{3,2,1,0:T(8,128)(2,1)S(1)}, bf16[1,8,16,128]{3,2,1,0:T(8,128)(2,1)S(1)}, u32[]{:S(2)}, u32[]{:S(2)}) collective-permute-start(bf16[1,8,16,128]{3,2,1,0:T(8,128)(2,1)S(1)} %get-tuple-element.127), channel_id=1, source_target_pairs={{16,0},{32,16},{48,32},{64,48},{80,64},{96,80},{112,96},{128,112},... | collective-permute-start | bytes 98312 | tf_op jit(solution)/shard_map/ppermute | solution.py:15
  77.7 10.1 %collective-permute-start.8 = (bf16[1,8,16,128]{3,2,1,0:T(8,128)(2,1)S(1)}, bf16[1,8,16,128]{3,2,1,0:T(8,128)(2,1)S(1)}, u32[]{:S(2)}, u32[]{:S(2)}) collective-permute-start(bf16[1,8,16,128]{3,2,1,0:T(8,128)(2,1)S(1)} %get-tuple-element.126), channel_id=1, source_target_pairs={{0,16},{16,32},{32,48},{48,64},{64,80},{80,96},{96,112},{112,128},... | collective-permute-start | bytes 98312 | tf_op jit(solution)/shard_map/ppermute | solution.py:14
  87.7 5.9 %collective-permute-start.11 = (bf16[6,1,16,128]{3,2,1,0:T(8,128)(2,1)S(1)}, bf16[6,1,16,128]{3,2,1,0:T(8,128)(2,1)S(1)}, u32[]{:S(2)}, u32[]{:S(2)}) collective-permute-start(bf16[6,1,16,128]{3,2,1,0:T(8,128)(2,1)S(1)} %get-tuple-element.121), channel_id=1, source_target_pairs={{1,0},{2,1},{3,2},{4,3},{5,4},{6,5},{7,6},{8,7},{9,8},{10,9},{11,1... | collective-permute-start | bytes 73736 | tf_op jit(solution)/shard_map/ppermute | solution.py:15
  89.7 7.8 %collective-permute-start.10 = (bf16[6,1,16,128]{3,2,1,0:T(8,128)(2,1)S(1)}, bf16[6,1,16,128]{3,2,1,0:T(8,128)(2,1)S(1)}, u32[]{:S(2)}, u32[]{:S(2)}) collective-permute-start(bf16[6,1,16,128]{3,2,1,0:T(8,128)(2,1)S(1)} %get-tuple-element.120), channel_id=1, source_target_pairs={{0,1},{1,2},{2,3},{3,4},{4,5},{5,6},{6,7},{7,8},{8,9},{9,10},{10,1... | collective-permute-start | bytes 73736 | tf_op jit(solution)/shard_map/ppermute | solution.py:14
  98.4 1.2 %copy-start.2 = (bf16[3456,128]{1,0:T(8,128)(2,1)S(1)}, bf16[3456,128]{1,0:T(8,128)(2,1)}, u32[]{:S(2)}) copy-start(bf16[3456,128]{1,0:T(8,128)(2,1)} %param.22) | copy-start | bytes 2654212
  100.9 0.7 copy-start.6
where the time goes:
time: 103 us; the launch traced here: 102 us
  starting transfers between devices  41.2 us (40%)
  waiting for transfers between devices  38.3 us (37%)
  local copies, waits for them, and re-layouts  12.1 us (12%)
  matrix products  7.36 us (7%)
  other arithmetic  2.32 us (2%)
    ppermute x6, waiting for transfers between devices, with_halo(): before = lax.ppermute(last, axis, up)  38.2 us
    ppermute x6, starting transfers between devices, with_halo(): after = lax.ppermute(leading, axis, down)  24.7 us
    ppermute x6, starting transfers between devices, with_halo(): before = lax.ppermute(last, axis, up)  16.5 us
    transpose x1, local copies, waits for them, and re-layouts, partial_upsample(): weight.reshape(64, in_width, out_width).transpose(1, 0, 2)  6.41 us
    dot_general x6, matrix products, conv_block(): jnp.dot(jnp.concatenate(slices, 1), kernel[step_x], preferred_element_typ...  3.8 us
    dot_general x1, matrix products, partial_upsample(): jnp.dot(coarse.reshape(-1, in_width), table, preferred_element_type=jnp.f...  3.56 us
    unnamed x61, local copies, waits for them, and re-layouts  3.25 us
  transfers between devices with their start and end apart: 12, of which 6 were waited for; matrix products, arithmetic and copies ran while one was open for 0% of the time, Pallas kernels for 0%

commit v1 on v0

v1 whole, which is shorter than its diff:
```python
import jax
import jax.numpy as jnp
from jax import lax
from jax.experimental import pallas as pl
from jax.experimental.pallas import tpu as pltpu
from jax.sharding import PartitionSpec as P

GX = 32
GY = 16
AXES = ("gx", "gy")
BF = jnp.bfloat16
F32 = jnp.float32
VMEM = pl.BlockSpec(memory_space=pltpu.VMEM)


def rank(x, y):
    return x * GY + y


NEAR = [(rank(x, y), rank(x ^ 1, y)) for x in range(GX) for y in range(GY)]
FAR = [
    (rank(x, y), rank(((x + 1) ^ 1) - 1, y)) for x in range(1, GX - 1) for y in range(GY)
]
UP = [(rank(x, y), rank(x, y + 1)) for x in range(GX) for y in range(GY - 1)]
DOWN = [(j, i) for i, j in UP]


def send(value, pairs):
    return lax.ppermute(value, AXES, pairs)


def pack_x_kernel(coarse, skip, far, near):
    odd = lax.axis_index("gx") % 2
    for half in range(2):
        block = coarse[:, half * 128 : half * 128 + 128]
        far[half * 64 : half * 64 + 64] = block
        near[half * 64 : half * 64 + 64] = block
    far[128:384] = skip[pl.ds(2 * odd, 2)].reshape(256, 128)
    near[128:384] = skip[pl.ds(2 - 2 * odd, 2)].reshape(256, 128)


def pack_x(coarse, skip):
    edge = jax.ShapeDtypeStruct((384, 128), BF)
    return pl.pallas_call(
        pack_x_kernel,
        out_shape=(edge, edge),
        in_specs=[VMEM, VMEM],
        out_specs=(VMEM, VMEM),
    )(coarse, skip)


def pack_y_kernel(coarse, skip, near, far, up, down):
    for out, first in ((down, 0), (up, 1)):
        for half in range(2):
            for x in range(2):
                row = half * 96 + x * 16
                at = x * 32 + first * 16
                out[row : row + 16] = coarse[at : at + 16, half * 128 : half * 128 + 128]
                for s, source in ((1, near), (2, far)):
                    row = half * 96 + s * 32 + x * 16
                    at = half * 64 + x * 32 + first * 16
                    out[row : row + 16] = source[at : at + 16]
        out[192:320] = skip[:, first * 6 : first * 6 + 2].reshape(128, 128)
        for s, source in ((0, near), (1, far)):
            for x in range(2):
                row = 320 + s * 64 + x * 32
                at = 128 + x * 128 + first * 96
                out[row : row + 32] = source[at : at + 32]


def pack_y(coarse, skip, near, far):
    edge = jax.ShapeDtypeStruct((448, 128), BF)
    return pl.pallas_call(
        pack_y_kernel,
        out_shape=(edge, edge),
        in_specs=[VMEM] * 4,
        out_specs=(VMEM, VMEM),
    )(coarse, skip, near, far)


TAPS = (((1, 1), (3, 0)), ((0, 2), (2, 1)))


def later(value):
    return jnp.concatenate([jnp.zeros_like(value[:, :1]), value[:, :-1]], 1)


def earlier(value):
    return jnp.concatenate([value[:, 1:], jnp.zeros_like(value[:, :1])], 1)


def main_kernel(
    coarse, skip, near, far, low, high, uw, ub, fw, fb, sw, sb, out, cells, joined, hidden, mixed
):
    gx = lax.axis_index("gx")
    gy = lax.axis_index("gy")
    odd = gx % 2
    near_c = 4 - 4 * odd
    far_c = 4 * odd
    near_f = 6 - 6 * odd
    far_f = 6 * odd
    for half in range(2):
        lanes = slice(half * 128, half * 128 + 128)
        cells[2:4, 2:6, :, lanes] = coarse[:, lanes].astype(F32).reshape(2, 4, 8, 128)
        for at, source in ((near_c, near), (far_c, far)):
            cells[pl.ds(at, 2), 2:6, :, lanes] = (
                source[half * 64 : half * 64 + 64].astype(F32).reshape(2, 4, 8, 128)
            )
        for at, source in ((0, low), (6, high)):
            for s, x in ((0, 2), (1, near_c), (2, far_c)):
                row = half * 96 + s * 32
                cells[pl.ds(x, 2), at : at + 2, :, lanes] = (
                    source[row : row + 32].astype(F32).reshape(2, 2, 8, 128)
                )
    joined[2:6, 2:10, :, 128:256] = skip[...]
    joined[pl.ds(near_f, 2), 2:10, :, 128:256] = near[128:384].reshape(2, 8, 16, 128)
    joined[pl.ds(far_f, 2), 2:10, :, 128:256] = far[128:384].reshape(2, 8, 16, 128)
    for at, source in ((0, low), (10, high)):
        joined[2:6, at : at + 2, :, 128:256] = source[192:320].reshape(4, 2, 16, 128)
        joined[pl.ds(near_f, 2), at : at + 2, :, 128:256] = source[320:384].reshape(2, 2, 16, 128)
        joined[pl.ds(far_f, 2), at : at + 2, :, 128:256] = source[384:448].reshape(2, 2, 16, 128)
    bias = ub[...]
    for px in range(2):
        for py in range(2):
            lhs = []
            rhs = []
            for kx, ix in TAPS[px]:
                for ky, iy in TAPS[py]:
                    block = cells[ix : ix + 4, iy : iy + 6]
                    lhs.append(block.reshape(192, 256).astype(BF))
                    at = kx * 16 + ky * 4
                    rhs.append(jnp.concatenate([uw[at + kz] for kz in range(4)], 1))
            terms = jnp.dot(
                jnp.concatenate(lhs, 1), jnp.concatenate(rhs, 0), preferred_element_type=F32
            ).reshape(24, 8, 512)
            even = terms[:, :, 128:256] + later(terms[:, :, 384:512]) + bias
            uneven = terms[:, :, 256:384] + earlier(terms[:, :, 0:128]) + bias
            mixed[:, pl.ds(0, 8, 2), :] = even
            mixed[:, pl.ds(1, 8, 2), :] = uneven
            for a in range(4):
                for b in range(6):
                    joined[2 * a + px, 2 * b + py, :, 0:128] = mixed[a * 6 + b].astype(BF)

    @pl.when(gx == 0)
    def _():
        joined[0:2, :, :, 0:128] = jnp.zeros((2, 12, 16, 128), BF)

    @pl.when(gx == GX - 1)
    def _():
        joined[6:8, :, :, 0:128] = jnp.zeros((2, 12, 16, 128), BF)

    @pl.when(gy == 0)
    def _():
        joined[:, 0:2, :, 0:128] = jnp.zeros((8, 2, 16, 128), BF)

    @pl.when(gy == GY - 1)
    def _():
        joined[:, 10:12, :, 0:128] = jnp.zeros((8, 2, 16, 128), BF)

    kernel = jnp.concatenate([fw[:, dz].reshape(2304, 128) for dz in range(3)], 1)
    for x in range(0, 6, 2):
        lhs = [
            joined[x + dx : x + dx + 2, dy : dy + 10].reshape(320, 256)
            for dx in range(3)
            for dy in range(3)
        ]
        terms = jnp.dot(jnp.concatenate(lhs, 1), kernel, preferred_element_type=F32)
        terms = terms.reshape(20, 16, 384)
        value = (
            terms[:, :, 128:256]
            + later(terms[:, :, 0:128])
            + earlier(terms[:, :, 256:384])
            + fb[...]
        )
        hidden[x : x + 2] = jnp.maximum(value, 0.0).astype(BF).reshape(2, 10, 16, 128)

    @pl.when(gx == 0)
    def _():
        hidden[0:1] = jnp.zeros((1, 10, 16, 128), BF)

    @pl.when(gx == GX - 1)
    def _():
        hidden[5:6] = jnp.zeros((1, 10, 16, 128), BF)

    @pl.when(gy == 0)
    def _():
        hidden[:, 0:1] = jnp.zeros((6, 1, 16, 128), BF)

    @pl.when(gy == GY - 1)
    def _():
        hidden[:, 9:10] = jnp.zeros((6, 1, 16, 128), BF)

    kernel = jnp.concatenate([sw[:, dz].reshape(1152, 128) for dz in range(3)], 1)
    for x in range(0, 4, 2):
        lhs = [
            hidden[x + dx : x + dx + 2, dy : dy + 8].reshape(256, 128)
            for dx in range(3)
            for dy in range(3)
        ]
        terms = jnp.dot(jnp.concatenate(lhs, 1), kernel, preferred_element_type=F32)
        terms = terms.reshape(16, 16, 384)
        value = (
            terms[:, :, 128:256]
            + later(terms[:, :, 0:128])
            + earlier(terms[:, :, 256:384])
            + sb[...]
        )
        out[x : x + 2] = value.astype(BF).reshape(2, 8, 16, 128)


def main(coarse, skip, near, far, low, high, uw, ub, fw, fb, sw, sb):
    return pl.pallas_call(
        main_kernel,
        out_shape=jax.ShapeDtypeStruct((4, 8, 16, 128), BF),
        in_specs=[VMEM] * 12,
        out_specs=VMEM,
        scratch_shapes=[
            pltpu.VMEM((6, 8, 8, 256), F32),
            pltpu.VMEM((8, 12, 16, 256), BF),
            pltpu.VMEM((6, 10, 16, 128), BF),
            pltpu.VMEM((24, 16, 128), F32),
        ],
        compiler_params=pltpu.CompilerParams(vmem_limit_bytes=40 * 1024 * 1024),
        cost_estimate=pl.CostEstimate(flops=3_000_000_000, bytes_accessed=8_000_000, transcendentals=0),
    )(coarse, skip, near, far, low, high, uw, ub, fw, fb, sw, sb)


def per_device(coarse, skip, up_weight, up_bias, first_weight, first_bias, second_weight, second_bias):
    coarse = coarse.reshape(64, 256)
    far, near = pack_x(coarse, skip)
    far = send(far, FAR)
    near = send(near, NEAR)
    up, down = pack_y(coarse, skip, near, far)
    low = send(up, UP)
    high = send(down, DOWN)
    return main(
        coarse,
        skip,
        near,
        far,
        low,
        high,
        up_weight.reshape(64, 256, 128),
        up_bias.reshape(1, 128),
        first_weight.reshape(9, 3, 256, 128),
        first_bias.reshape(1, 128),
        second_weight.reshape(9, 3, 128, 128),
        second_bias.reshape(1, 128),
    )


def solution(mesh):
    return jax.shard_map(
        per_device,
        mesh=mesh,
        in_specs=(P("gx", "gy"), P("gx", "gy"), P(), P(), P(), P(), P(), P()),
        out_specs=P("gx", "gy"),
        check_vma=False,
    )
```

time: 103 us -> 51.4 us (0.50)
  the two profiles are of different devices: /device:TPU:38 before, /device:TPU:30 now
where the time goes in v1:
time: 51.4 us; the launch traced here: 50.9 us
  starting transfers between devices  20.8 us (40%)
  local copies, waits for them, and re-layouts  10.9 us (21%)
  waiting for transfers between devices  10.7 us (21%)
  Pallas kernels  8.4 us (16%)
    ppermute x4, starting transfers between devices, send(): return lax.ppermute(value, AXES, pairs)  20.8 us
    unnamed x24, local copies, waits for them, and re-layouts  10.9 us
    ppermute x4, waiting for transfers between devices, send(): return lax.ppermute(value, AXES, pairs)  10.7 us
    pallas_call x1, Pallas kernels, main(): pl.pallas_call(main_kernel, out_shape=jax.ShapeDtypeStruct((4, 8, 16, 128...  5.06 us
    pallas_call x1, Pallas kernels, pack_y(): pl.pallas_call(pack_y_kernel, out_shape=(edge, edge), in_specs=[VMEM] * 4...  1.72 us
    pallas_call x1, Pallas kernels, pack_x(): pl.pallas_call(pack_x_kernel, out_shape=(edge, edge), in_specs=[VMEM, VME...  1.62 us
  transfers between devices with their start and end apart: 4, of which 3 were waited for; matrix products, arithmetic and copies ran while one was open for 0% of the time, Pallas kernels for 0%

profile of v1, /device:TPU:30, one launch (start us, length us, event | category | flops | bytes accessed | tf_op | source)
XLA Modules:
  0.0 50.9 jit_solution(12460444609811558033)
XLA Ops:
  0.0 1.6 %shard_map.82 = (bf16[384,128]{1,0:T(8,128)(2,1)}, bf16[384,128]{1,0:T(8,128)(2,1)}) custom-call(bf16[64,256]{1,0:T(8,128)(2,1)} %bitcast.7, bf16[4,8,16,128]{3,2,1,0:T(8,128)(2,1)} %skip.5), custom_call_target="tpu_custom_call" | custom-call | tf_op jit(solution)/shard_map/pallas_call | solution.py:44
  1.6 1.9 %collective-permute-start = (bf16[384,128]{1,0:T(8,128)(2,1)}, bf16[384,128]{1,0:T(8,128)(2,1)S(1)}, u32[]{:S(2)}, u32[]{:S(2)}) collective-permute-start(bf16[384,128]{1,0:T(8,128)(2,1)} %get-tuple-element.9), channel_id=1, source_target_pairs={{0,16},{1,17},{2,18},{3,19},{4,20},{5,21},{6,22},{7,23},{8,24},{9,... | collective-permute-start | bytes 294920 | tf_op jit(solution)/shard_map/ppermute | solution.py:29
  3.5 13.1 %collective-permute-start.1 = (bf16[384,128]{1,0:T(8,128)(2,1)}, bf16[384,128]{1,0:T(8,128)(2,1)S(1)}, u32[]{:S(2)}, u32[]{:S(2)}) collective-permute-start(bf16[384,128]{1,0:T(8,128)(2,1)} %get-tuple-element.10), channel_id=1, source_target_pairs={{16,32},{17,33},{18,34},{19,35},{20,36},{21,37},{22,38},{23,39},{2... | collective-permute-start | bytes 294920 | tf_op jit(solution)/shard_map/ppermute | solution.py:29
  16.6 0.0 collective-permute-done.near
  16.7 0.0 copy-start.2
  16.7 5.6 %collective-permute-done.1.far = bf16[384,128]{1,0:T(8,128)(2,1)S(1)} collective-permute-done((bf16[384,128]{1,0:T(8,128)(2,1)}, bf16[384,128]{1,0:T(8,128)(2,1)S(1)}, u32[]{:S(2)}, u32[]{:S(2)}) %collective-permute-start.1) | collective-permute-done | bytes 98336 | tf_op jit(solution)/shard_map/ppermute | solution.py:29
  22.3 0.0 copy-done.2
  22.3 0.0 copy-start.4
  22.3 0.6 %copy-done.4 = bf16[384,128]{1,0:T(8,128)(2,1)} copy-done((bf16[384,128]{1,0:T(8,128)(2,1)}, bf16[384,128]{1,0:T(8,128)(2,1)S(1)}, u32[]{:S(2)}) %copy-start.4) | copy-done | bytes 98328
  22.9 1.7 %shard_map.83 = (bf16[448,128]{1,0:T(8,128)(2,1)}, bf16[448,128]{1,0:T(8,128)(2,1)}) custom-call(bf16[64,256]{1,0:T(8,128)(2,1)} %bitcast.8, bf16[4,8,16,128]{3,2,1,0:T(8,128)(2,1)} %skip.5, bf16[384,128]{1,0:T(8,128)(2,1)} %copy-done.2, bf16[384,128]{1,0:T(8,128)(2,1)} %copy-done.4), custom_call_target="tpu_custom_call" | custom-call | tf_op jit(solution)/shard_map/pallas_call | solution.py:73
  24.6 1.9 %collective-permute-start.2 = (bf16[448,128]{1,0:T(8,128)(2,1)}, bf16[448,128]{1,0:T(8,128)(2,1)S(1)}, u32[]{:S(2)}, u32[]{:S(2)}) collective-permute-start(bf16[448,128]{1,0:T(8,128)(2,1)} %get-tuple-element.11), channel_id=1, source_target_pairs={{0,1},{1,2},{2,3},{3,4},{4,5},{5,6},{6,7},{7,8},{8,9},{9,10},{10,1... | collective-permute-start | bytes 344072 | tf_op jit(solution)/shard_map/ppermute | solution.py:29
  26.6 3.9 %collective-permute-start.3 = (bf16[448,128]{1,0:T(8,128)(2,1)}, bf16[448,128]{1,0:T(8,128)(2,1)S(1)}, u32[]{:S(2)}, u32[]{:S(2)}) collective-permute-start(bf16[448,128]{1,0:T(8,128)(2,1)} %get-tuple-element.12), channel_id=1, source_target_pairs={{1,0},{2,1},{3,2},{4,3},{5,4},{6,5},{7,6},{8,7},{9,8},{10,9},{11,1... | collective-permute-start | bytes 344072 | tf_op jit(solution)/shard_map/ppermute | solution.py:29
  30.5 1.0 %collective-permute-done.2.low = bf16[448,128]{1,0:T(8,128)(2,1)S(1)} collective-permute-done((bf16[448,128]{1,0:T(8,128)(2,1)}, bf16[448,128]{1,0:T(8,128)(2,1)S(1)}, u32[]{:S(2)}, u32[]{:S(2)}) %collective-permute-start.2) | collective-permute-done | bytes 114720 | tf_op jit(solution)/shard_map/ppermute | solution.py:29
  31.5 4.0 %collective-permute-done.3.high = bf16[448,128]{1,0:T(8,128)(2,1)S(1)} collective-permute-done((bf16[448,128]{1,0:T(8,128)(2,1)}, bf16[448,128]{1,0:T(8,128)(2,1)S(1)}, u32[]{:S(2)}, u32[]{:S(2)}) %collective-permute-start.3) | collective-permute-done | bytes 114720 | tf_op jit(solution)/shard_map/ppermute | solution.py:29
  35.6 0.0 copy-start
  35.6 0.9 %copy-done = bf16[4,8,16,128]{3,2,1,0:T(8,128)(2,1)S(1)} copy-done((bf16[4,8,16,128]{3,2,1,0:T(8,128)(2,1)S(1)}, bf16[4,8,16,128]{3,2,1,0:T(8,128)(2,1)}, u32[]{:S(2)}) %copy-start) | copy-done | bytes 131096
  36.5 0.0 copy-start.1
  36.5 0.8 %copy-done.1 = bf16[2,4,8,256]{3,2,1,0:T(8,128)(2,1)S(1)} copy-done((bf16[2,4,8,256]{3,2,1,0:T(8,128)(2,1)S(1)}, bf16[2,4,8,256]{3,2,1,0:T(8,128)(2,1)}, u32[]{:S(2)}) %copy-start.1) | copy-done | bytes 32792
  37.2 0.0 copy-start.3
  37.2 0.9 %copy-done.3 = bf16[384,128]{1,0:T(8,128)(2,1)S(1)} copy-done((bf16[384,128]{1,0:T(8,128)(2,1)S(1)}, bf16[384,128]{1,0:T(8,128)(2,1)}, u32[]{:S(2)}) %copy-start.3) | copy-done | bytes 98328
  38.1 0.0 copy-start.5
  38.1 0.9 %copy-done.5 = bf16[384,128]{1,0:T(8,128)(2,1)S(1)} copy-done((bf16[384,128]{1,0:T(8,128)(2,1)S(1)}, bf16[384,128]{1,0:T(8,128)(2,1)}, u32[]{:S(2)}) %copy-start.5) | copy-done | bytes 98328
  39.0 0.0 copy-start.6
  39.0 2.2 %copy-done.6 = bf16[16384,128]{1,0:T(8,128)(2,1)S(1)} copy-done((bf16[16384,128]{1,0:T(8,128)(2,1)S(1)}, bf16[16384,128]{1,0:T(8,128)(2,1)}, u32[]{:S(2)}) %copy-start.6) | copy-done | bytes 4194328
  41.2 0.0 copy-start.7
  41.2 1.5 %copy-done.7 = bf16[6912,128]{1,0:T(8,128)(2,1)S(1)} copy-done((bf16[6912,128]{1,0:T(8,128)(2,1)S(1)}, bf16[6912,128]{1,0:T(8,128)(2,1)}, u32[]{:S(2)}) %copy-start.7) | copy-done | bytes 1769496
  42.7 0.0 copy-start.8
  42.7 1.2 %copy-done.8 = bf16[3456,128]{1,0:T(8,128)(2,1)S(1)} copy-done((bf16[3456,128]{1,0:T(8,128)(2,1)S(1)}, bf16[3456,128]{1,0:T(8,128)(2,1)}, u32[]{:S(2)}) %copy-start.8) | copy-done | bytes 884760
  43.9 0.7 %copy-done.9 = f32[128]{0:T(128)S(1)} copy-done((f32[128]{0:T(128)S(1)}, f32[128]{0:T(128)}, u32[]{:S(2)}) %copy-start.9) | copy-done | bytes 536
  44.5 0.7 %copy-done.10 = f32[128]{0:T(128)S(1)} copy-done((f32[128]{0:T(128)S(1)}, f32[128]{0:T(128)}, u32[]{:S(2)}) %copy-start.10) | copy-done | bytes 536
  45.2 0.7 %copy-done.11 = f32[128]{0:T(128)S(1)} copy-done((f32[128]{0:T(128)S(1)}, f32[128]{0:T(128)}, u32[]{:S(2)}) %copy-start.11) | copy-done | bytes 536
  45.8 5.1 %shard_map.84 = bf16[4,8,16,128]{3,2,1,0:T(8,128)(2,1)} custom-call(bf16[64,256]{1,0:T(8,128)(2,1)S(1)} %bitcast.9, bf16[4,8,16,128]{3,2,1,0:T(8,128)(2,1)S(1)} %copy-done, bf16[384,128]{1,0:T(8,128)(2,1)S(1)} %copy-done.3, bf16[384,128]{1,0:T(8,128)(2,1)S(1)} %copy-done.5, bf16[448,128]{1,0:T(8,128)(2,1)S(1)} %collective-permute-done.2.low, ...), custom_call_target="tpu_custom_call" | custom-call | flops 3000000000 | bytes 8000000 | tf_op jit(solution)/shard_map/pallas_call | solution.py:212
  (3 shorter events, 0.0 us)
Async XLA Ops:
  1.6 15.0 %collective-permute-start = (bf16[384,128]{1,0:T(8,128)(2,1)}, bf16[384,128]{1,0:T(8,128)(2,1)S(1)}, u32[]{:S(2)}, u32[]{:S(2)}) collective-permute-start(bf16[384,128]{1,0:T(8,128)(2,1)} %get-tuple-element.9), channel_id=1, source_target_pairs={{0,16},{1,17},{2,18},{3,19},{4,20},{5,21},{6,22},{7,23},{8,24},{9,... | collective-permute-start | bytes 294920 | tf_op jit(solution)/shard_map/ppermute | solution.py:29
  3.5 18.7 %collective-permute-start.1 = (bf16[384,128]{1,0:T(8,128)(2,1)}, bf16[384,128]{1,0:T(8,128)(2,1)S(1)}, u32[]{:S(2)}, u32[]{:S(2)}) collective-permute-start(bf16[384,128]{1,0:T(8,128)(2,1)} %get-tuple-element.10), channel_id=1, source_target_pairs={{16,32},{17,33},{18,34},{19,35},{20,36},{21,37},{22,38},{23,39},{2... | collective-permute-start | bytes 294920 | tf_op jit(solution)/shard_map/ppermute | solution.py:29
  16.7 5.6 %copy-start.2 = (bf16[384,128]{1,0:T(8,128)(2,1)}, bf16[384,128]{1,0:T(8,128)(2,1)S(1)}, u32[]{:S(2)}) copy-start(bf16[384,128]{1,0:T(8,128)(2,1)S(1)} %collective-permute-done.near) | copy-start | bytes 294916
  22.3 0.6 %copy-start.4 = (bf16[384,128]{1,0:T(8,128)(2,1)}, bf16[384,128]{1,0:T(8,128)(2,1)S(1)}, u32[]{:S(2)}) copy-start(bf16[384,128]{1,0:T(8,128)(2,1)S(1)} %collective-permute-done.1.far) | copy-start | bytes 294916
  24.6 6.9 %collective-permute-start.2 = (bf16[448,128]{1,0:T(8,128)(2,1)}, bf16[448,128]{1,0:T(8,128)(2,1)S(1)}, u32[]{:S(2)}, u32[]{:S(2)}) collective-permute-start(bf16[448,128]{1,0:T(8,128)(2,1)} %get-tuple-element.11), channel_id=1, source_target_pairs={{0,1},{1,2},{2,3},{3,4},{4,5},{5,6},{6,7},{7,8},{8,9},{9,10},{10,1... | collective-permute-start | bytes 344072 | tf_op jit(solution)/shard_map/ppermute | solution.py:29
  26.6 9.0 %collective-permute-start.3 = (bf16[448,128]{1,0:T(8,128)(2,1)}, bf16[448,128]{1,0:T(8,128)(2,1)S(1)}, u32[]{:S(2)}, u32[]{:S(2)}) collective-permute-start(bf16[448,128]{1,0:T(8,128)(2,1)} %get-tuple-element.12), channel_id=1, source_target_pairs={{1,0},{2,1},{3,2},{4,3},{5,4},{6,5},{7,6},{8,7},{9,8},{10,9},{11,1... | collective-permute-start | bytes 344072 | tf_op jit(solution)/shard_map/ppermute | solution.py:29
  35.6 0.9 %copy-start = (bf16[4,8,16,128]{3,2,1,0:T(8,128)(2,1)S(1)}, bf16[4,8,16,128]{3,2,1,0:T(8,128)(2,1)}, u32[]{:S(2)}) copy-start(bf16[4,8,16,128]{3,2,1,0:T(8,128)(2,1)} %skip.5) | copy-start | bytes 393220
  36.5 0.8 %copy-start.1 = (bf16[2,4,8,256]{3,2,1,0:T(8,128)(2,1)S(1)}, bf16[2,4,8,256]{3,2,1,0:T(8,128)(2,1)}, u32[]{:S(2)}) copy-start(bf16[2,4,8,256]{3,2,1,0:T(8,128)(2,1)} %param.8) | copy-start | bytes 98308
  37.2 0.9 %copy-start.3 = (bf16[384,128]{1,0:T(8,128)(2,1)S(1)}, bf16[384,128]{1,0:T(8,128)(2,1)}, u32[]{:S(2)}) copy-start(bf16[384,128]{1,0:T(8,128)(2,1)} %copy-done.2) | copy-start | bytes 294916
  38.1 0.9 %copy-start.5 = (bf16[384,128]{1,0:T(8,128)(2,1)S(1)}, bf16[384,128]{1,0:T(8,128)(2,1)}, u32[]{:S(2)}) copy-start(bf16[384,128]{1,0:T(8,128)(2,1)} %copy-done.4) | copy-start | bytes 294916
  39.0 2.2 %copy-start.6 = (bf16[16384,128]{1,0:T(8,128)(2,1)S(1)}, bf16[16384,128]{1,0:T(8,128)(2,1)}, u32[]{:S(2)}) copy-start(bf16[16384,128]{1,0:T(8,128)(2,1)} %param.10) | copy-start | bytes 12582916
  41.2 1.5 %copy-start.7 = (bf16[6912,128]{1,0:T(8,128)(2,1)S(1)}, bf16[6912,128]{1,0:T(8,128)(2,1)}, u32[]{:S(2)}) copy-start(bf16[6912,128]{1,0:T(8,128)(2,1)} %param.12) | copy-start | bytes 5308420
  42.7 1.2 %copy-start.8 = (bf16[3456,128]{1,0:T(8,128)(2,1)S(1)}, bf16[3456,128]{1,0:T(8,128)(2,1)}, u32[]{:S(2)}) copy-start(bf16[3456,128]{1,0:T(8,128)(2,1)} %param.14) | copy-start | bytes 2654212
  43.8 0.7 %copy-start.9 = (f32[128]{0:T(128)S(1)}, f32[128]{0:T(128)}, u32[]{:S(2)}) copy-start(f32[128]{0:T(128)} %param.11) | copy-start | bytes 1540
  44.5 0.7 %copy-start.10 = (f32[128]{0:T(128)S(1)}, f32[128]{0:T(128)}, u32[]{:S(2)}) copy-start(f32[128]{0:T(128)} %param.13) | copy-start | bytes 1540
  45.2 0.7 %copy-start.11 = (f32[128]{0:T(128)S(1)}, f32[128]{0:T(128)}, u32[]{:S(2)}) copy-start(f32[128]{0:T(128)} %param.15) | copy-start | bytes 1540

commit v2 on v1

--- a/solution.py
+++ b/solution.py
@@ -11,6 +11,16 @@
 BF = jnp.bfloat16
 F32 = jnp.float32
 VMEM = pl.BlockSpec(memory_space=pltpu.VMEM)
+HBM = pl.BlockSpec(memory_space=pltpu.HBM)
+SMALL = 4 * 1024 * 1024
+
+
+def in_hbm(value):
+    return pltpu.with_memory_space_constraint(value, pltpu.HBM)
+
+
+def in_vmem(value):
+    return pltpu.VMEM(value.shape, value.dtype)
 
 
 def rank(x, y):
@@ -29,27 +39,68 @@
     return lax.ppermute(value, AXES, pairs)
 
 
-def pack_x_kernel(coarse, skip, far, near):
+def fill_x(edge, coarse, skip, first):
+    for half in range(2):
+        edge[half * 64 : half * 64 + 64] = coarse[:, half * 128 : half * 128 + 128]
+    edge[128:384] = skip[pl.ds(first, 2)].reshape(256, 128)
+
+
+def fields_kernel(coarse_in, skip_in, coarse, skip, far, sems):
     odd = lax.axis_index("gx") % 2
-    for half in range(2):
-        block = coarse[:, half * 128 : half * 128 + 128]
-        far[half * 64 : half * 64 + 64] = block
-        near[half * 64 : half * 64 + 64] = block
-    far[128:384] = skip[pl.ds(2 * odd, 2)].reshape(256, 128)
-    near[128:384] = skip[pl.ds(2 - 2 * odd, 2)].reshape(256, 128)
-
-
-def pack_x(coarse, skip):
-    edge = jax.ShapeDtypeStruct((384, 128), BF)
+    copies = [
+        pltpu.make_async_copy(coarse_in, coarse, sems.at[0]),
+        pltpu.make_async_copy(skip_in, skip, sems.at[1]),
+    ]
+    for copy in copies:
+        copy.start()
+    for copy in copies:
+        copy.wait()
+    fill_x(far, coarse, skip, 2 * odd)
+
+
+def fields(coarse, skip):
     return pl.pallas_call(
-        pack_x_kernel,
-        out_shape=(edge, edge),
-        in_specs=[VMEM, VMEM],
-        out_specs=(VMEM, VMEM),
-    )(coarse, skip)
-
-
-def pack_y_kernel(coarse, skip, near, far, up, down):
+        fields_kernel,
+        out_shape=(
+            in_vmem(coarse),
+            in_vmem(skip),
+            pltpu.VMEM((384, 128), BF),
+        ),
+        in_specs=[HBM, HBM],
+        out_specs=[VMEM] * 3,
+        scratch_shapes=[pltpu.SemaphoreType.DMA((2,))],
+        compiler_params=pltpu.CompilerParams(vmem_limit_bytes=SMALL),
+    )(in_hbm(coarse), in_hbm(skip))
+
+
+def stage_kernel(*refs):
+    sources, coarse, skip = refs[:6], refs[6], refs[7]
+    targets, near, sems = refs[8:14], refs[14], refs[15]
+    odd = lax.axis_index("gx") % 2
+    copies = [
+        pltpu.make_async_copy(source, target, sems.at[i])
+        for i, (source, target) in enumerate(zip(sources, targets))
+    ]
+    for copy in copies:
+        copy.start()
+    fill_x(near, coarse, skip, 2 - 2 * odd)
+    for copy in copies:
+        copy.wait()
+
+
+def stage(weights, coarse, skip):
+    return pl.pallas_call(
+        stage_kernel,
+        out_shape=[in_vmem(w) for w in weights] + [pltpu.VMEM((384, 128), BF)],
+        in_specs=[HBM] * 6 + [VMEM] * 2,
+        out_specs=[VMEM] * 7,
+        scratch_shapes=[pltpu.SemaphoreType.DMA((6,))],
+        compiler_params=pltpu.CompilerParams(vmem_limit_bytes=SMALL),
+        cost_estimate=pl.CostEstimate(flops=0, bytes_accessed=14_000_000, transcendentals=0),
+    )(*[in_hbm(w) for w in weights], coarse, skip)
+
+
+def pack_y_kernel(coarse, skip, far, near, up, down):
     for out, first in ((down, 0), (up, 1)):
         for half in range(2):
             for x in range(2):
@@ -68,14 +119,15 @@
                 out[row : row + 32] = source[at : at + 32]
 
 
-def pack_y(coarse, skip, near, far):
+def pack_y(coarse, skip, far, near):
     edge = jax.ShapeDtypeStruct((448, 128), BF)
     return pl.pallas_call(
         pack_y_kernel,
         out_shape=(edge, edge),
         in_specs=[VMEM] * 4,
         out_specs=(VMEM, VMEM),
-    )(coarse, skip, near, far)
+        compiler_params=pltpu.CompilerParams(vmem_limit_bytes=SMALL),
+    )(coarse, skip, far, near)
 
 
 TAPS = (((1, 1), (3, 0)), ((0, 2), (2, 1)))
@@ -220,26 +272,15 @@
             pltpu.VMEM((6, 10, 16, 128), BF),
             pltpu.VMEM((24, 16, 128), F32),
         ],
-        compiler_params=pltpu.CompilerParams(vmem_limit_bytes=40 * 1024 * 1024),
+        compiler_params=pltpu.CompilerParams(vmem_limit_bytes=24 * 1024 * 1024),
         cost_estimate=pl.CostEstimate(flops=3_000_000_000, bytes_accessed=8_000_000, transcendentals=0),
     )(coarse, skip, near, far, low, high, uw, ub, fw, fb, sw, sb)
 
 
 def per_device(coarse, skip, up_weight, up_bias, first_weight, first_bias, second_weight, second_bias):
-    coarse = coarse.reshape(64, 256)
-    far, near = pack_x(coarse, skip)
+    coarse, skip, far = fields(coarse.reshape(64, 256), skip)
     far = send(far, FAR)
-    near = send(near, NEAR)
-    up, down = pack_y(coarse, skip, near, far)
-    low = send(up, UP)
-    high = send(down, DOWN)
-    return main(
-        coarse,
-        skip,
-        near,
-        far,
-        low,
-        high,
+    weights = (
         up_weight.reshape(64, 256, 128),
         up_bias.reshape(1, 128),
         first_weight.reshape(9, 3, 256, 128),
@@ -247,6 +288,12 @@
         second_weight.reshape(9, 3, 128, 128),
         second_bias.reshape(1, 128),
     )
+    *weights, near = stage(weights, coarse, skip)
+    near = send(near, NEAR)
+    up, down = pack_y(coarse, skip, far, near)
+    low = send(up, UP)
+    high = send(down, DOWN)
+    return main(coarse, skip, near, far, low, high, *weights)
 
 
 def solution(mesh):

time: 51.4 us -> 36.5 us (0.71)
  local copies, waits for them, and re-layouts: 10.9 us -> 0 us
  waiting for transfers between devices: 10.7 us -> 6.93 us
  Pallas kernels: 8.4 us -> 9.07 us
  starting transfers between devices: 20.8 us -> 20.2 us
    unnamed x24 -> x0, local copies, waits for them, and re-layouts: 10.9 us -> none
    ppermute x4, waiting for transfers between devices: 10.7 us -> 6.93 us  [send(): return lax.ppermute(value, AXES, pairs)]
    pallas_call x1 -> x2, Pallas kernels: 1.62 us -> 3.99 us  [the longest x1 3.04 us: stage(): pl.pallas_call(stage_kernel, out_shape=[in_vmem(w) for w in weights] + [p...]
    pallas_call x1, Pallas kernels: 1.72 us -> 0.02 us  [pack_y(): pl.pallas_call(pack_y_kernel, out_shape=(edge, edge), in_specs=[VMEM] * 4...]
    ppermute x4, starting transfers between devices: 20.8 us -> 20.2 us  [send(): return lax.ppermute(value, AXES, pairs)]
  transfers between devices with their start and end apart: 4 -> 4, of which waited for: 3 -> 4; matrix products, arithmetic and copies ran while one was open for 0% -> 0% of each run, Pallas kernels for 0% -> 8%
where the time goes in v2:
time: 36.5 us; the launch traced here: 36.3 us
  starting transfers between devices  20.2 us (55%)
  Pallas kernels  9.07 us (25%)
  waiting for transfers between devices  6.93 us (19%)
    ppermute x4, starting transfers between devices, send(): return lax.ppermute(value, AXES, pairs)  20.2 us
    ppermute x4, waiting for transfers between devices, send(): return lax.ppermute(value, AXES, pairs)  6.93 us
    pallas_call x1, Pallas kernels, main(): pl.pallas_call(main_kernel, out_shape=jax.ShapeDtypeStruct((4, 8, 16, 128...  5.06 us
    pallas_call x1, Pallas kernels, stage(): pl.pallas_call(stage_kernel, out_shape=[in_vmem(w) for w in weights] + [p...  3.04 us
    pallas_call x1, Pallas kernels, fields(): pl.pallas_call(fields_kernel, out_shape=(in_vmem(coarse), in_vmem(skip),...  0.95 us
  transfers between devices with their start and end apart: 4, of which 4 were waited for; matrix products, arithmetic and copies ran while one was open for 0% of the time, Pallas kernels for 8%

profile of v2, /device:TPU:30, one launch (start us, length us, event | category | flops | bytes accessed | tf_op | source)
XLA Modules:
  0.0 36.3 jit_solution(14106953284589099180)
XLA Ops:
  0.0 0.9 %shard_map.82 = (bf16[64,256]{1,0:T(8,128)(2,1)S(1)}, bf16[4,8,16,128]{3,2,1,0:T(8,128)(2,1)S(1)}, bf16[384,128]{1,0:T(8,128)(2,1)S(1)}) custom-call(bf16[64,256]{1,0:T(8,128)(2,1)} %bitcast.10, bf16[4,8,16,128]{3,2,1,0:T(8,128)(2,1)} %skip_in.1), custom_call_target="tpu_custom_call" | custom-call | tf_op jit(solution)/shard_map/pallas_call | solution.py:62
  1.0 12.4 %collective-permute-start.1 = (bf16[384,128]{1,0:T(8,128)(2,1)S(1)}, bf16[384,128]{1,0:T(8,128)(2,1)S(1)}, u32[]{:S(2)}, u32[]{:S(2)}) collective-permute-start(bf16[384,128]{1,0:T(8,128)(2,1)S(1)} %get-tuple-element.20), channel_id=1, source_target_pairs={{16,32},{17,33},{18,34},{19,35},{20,36},{21,37},{22,38},{23,39},{2... | collective-permute-start | bytes 294920 | tf_op jit(solution)/shard_map/ppermute | solution.py:39
  13.4 3.0 %shard_map.83 = (bf16[64,256,128]{2,1,0:T(8,128)(2,1)S(1)}, f32[1,128]{1,0:T(1,128)S(1)}, bf16[9,3,256,128]{3,2,1,0:T(8,128)(2,1)S(1)}, f32[1,128]{1,0:T(1,128)S...) custom-call(bf16[64,256,128]{2,1,0:T(8,128)(2,1)} %bitcast.7, ...), custom_call_target="tpu_custom_call" | custom-call | bytes 14000000 | tf_op jit(solution)/shard_map/pallas_call | solution.py:92
  16.5 1.9 %collective-permute-start = (bf16[384,128]{1,0:T(8,128)(2,1)S(1)}, bf16[384,128]{1,0:T(8,128)(2,1)S(1)}, u32[]{:S(2)}, u32[]{:S(2)}) collective-permute-start(bf16[384,128]{1,0:T(8,128)(2,1)S(1)} %get-tuple-element.19), channel_id=1, source_target_pairs={{0,16},{1,17},{2,18},{3,19},{4,20},{5,21},{6,22},{7,23},{8,24},{9,... | collective-permute-start | bytes 294920 | tf_op jit(solution)/shard_map/ppermute | solution.py:39
  18.4 0.3 collective-permute-done.1.far
  18.7 0.9 %collective-permute-done.near = bf16[384,128]{1,0:T(8,128)(2,1)S(1)} collective-permute-done((bf16[384,128]{1,0:T(8,128)(2,1)S(1)}, bf16[384,128]{1,0:T(8,128)(2,1)S(1)}, u32[]{:S(2)}, u32[]{:S(2)}) %collective-permute-start) | collective-permute-done | bytes 98336 | tf_op jit(solution)/shard_map/ppermute | solution.py:39
  19.7 2.6 %collective-permute-start.2 = (bf16[448,128]{1,0:T(8,128)(2,1)S(1)}, bf16[448,128]{1,0:T(8,128)(2,1)S(1)}, u32[]{:S(2)}, u32[]{:S(2)}) collective-permute-start(bf16[448,128]{1,0:T(8,128)(2,1)S(1)} %get-tuple-element.21), channel_id=1, source_target_pairs={{0,1},{1,2},{2,3},{3,4},{4,5},{5,6},{6,7},{7,8},{8,9},{9,10},{10,1... | collective-permute-start | bytes 344072 | tf_op jit(solution)/shard_map/ppermute | solution.py:39
  22.3 3.3 %collective-permute-start.3 = (bf16[448,128]{1,0:T(8,128)(2,1)S(1)}, bf16[448,128]{1,0:T(8,128)(2,1)S(1)}, u32[]{:S(2)}, u32[]{:S(2)}) collective-permute-start(bf16[448,128]{1,0:T(8,128)(2,1)S(1)} %get-tuple-element.22), channel_id=1, source_target_pairs={{1,0},{2,1},{3,2},{4,3},{5,4},{6,5},{7,6},{8,7},{9,8},{10,9},{11,1... | collective-permute-start | bytes 344072 | tf_op jit(solution)/shard_map/ppermute | solution.py:39
  25.5 1.2 %collective-permute-done.2.low = bf16[448,128]{1,0:T(8,128)(2,1)S(1)} collective-permute-done((bf16[448,128]{1,0:T(8,128)(2,1)S(1)}, bf16[448,128]{1,0:T(8,128)(2,1)S(1)}, u32[]{:S(2)}, u32[]{:S(2)}) %collective-permute-start.2) | collective-permute-done | bytes 114720 | tf_op jit(solution)/shard_map/ppermute | solution.py:39
  26.8 4.4 %collective-permute-done.3.high = bf16[448,128]{1,0:T(8,128)(2,1)S(1)} collective-permute-done((bf16[448,128]{1,0:T(8,128)(2,1)S(1)}, bf16[448,128]{1,0:T(8,128)(2,1)S(1)}, u32[]{:S(2)}, u32[]{:S(2)}) %collective-permute-start.3) | collective-permute-done | bytes 114720 | tf_op jit(solution)/shard_map/ppermute | solution.py:39
  31.2 5.1 %shard_map.85 = bf16[4,8,16,128]{3,2,1,0:T(8,128)(2,1)} custom-call(bf16[64,256]{1,0:T(8,128)(2,1)S(1)} %get-tuple-element.17.refs_6_.coarse, bf16[4,8,16,128]{3,2,1,0:T(8,128)(2,1)S(1)} %get-tuple-element.18.refs_7_.skip, bf16[384,128]{1,0:T(8,128)(2,1)S(1)} %collective-permute-done.near, bf16[384,128]{1,0:T(8,128)(2,1)S(1)} %collective-permute-done.1.far, ...), custom_call_target="tpu_custom_call" | custom-call | flops 3000000000 | bytes 8000000 | tf_op jit(solution)/shard_map/pallas_call | solution.py:264
  (1 shorter events, 0.0 us)
Async XLA Ops:
  1.0 17.8 %collective-permute-start.1 = (bf16[384,128]{1,0:T(8,128)(2,1)S(1)}, bf16[384,128]{1,0:T(8,128)(2,1)S(1)}, u32[]{:S(2)}, u32[]{:S(2)}) collective-permute-start(bf16[384,128]{1,0:T(8,128)(2,1)S(1)} %get-tuple-element.20), channel_id=1, source_target_pairs={{16,32},{17,33},{18,34},{19,35},{20,36},{21,37},{22,38},{23,39},{2... | collective-permute-start | bytes 294920 | tf_op jit(solution)/shard_map/ppermute | solution.py:39
  16.5 3.2 %collective-permute-start = (bf16[384,128]{1,0:T(8,128)(2,1)S(1)}, bf16[384,128]{1,0:T(8,128)(2,1)S(1)}, u32[]{:S(2)}, u32[]{:S(2)}) collective-permute-start(bf16[384,128]{1,0:T(8,128)(2,1)S(1)} %get-tuple-element.19), channel_id=1, source_target_pairs={{0,16},{1,17},{2,18},{3,19},{4,20},{5,21},{6,22},{7,23},{8,24},{9,... | collective-permute-start | bytes 294920 | tf_op jit(solution)/shard_map/ppermute | solution.py:39
  19.7 7.1 %collective-permute-start.2 = (bf16[448,128]{1,0:T(8,128)(2,1)S(1)}, bf16[448,128]{1,0:T(8,128)(2,1)S(1)}, u32[]{:S(2)}, u32[]{:S(2)}) collective-permute-start(bf16[448,128]{1,0:T(8,128)(2,1)S(1)} %get-tuple-element.21), channel_id=1, source_target_pairs={{0,1},{1,2},{2,3},{3,4},{4,5},{5,6},{6,7},{7,8},{8,9},{9,10},{10,1... | collective-permute-start | bytes 344072 | tf_op jit(solution)/shard_map/ppermute | solution.py:39
  22.3 8.9 %collective-permute-start.3 = (bf16[448,128]{1,0:T(8,128)(2,1)S(1)}, bf16[448,128]{1,0:T(8,128)(2,1)S(1)}, u32[]{:S(2)}, u32[]{:S(2)}) collective-permute-start(bf16[448,128]{1,0:T(8,128)(2,1)S(1)} %get-tuple-element.22), channel_id=1, source_target_pairs={{1,0},{2,1},{3,2},{4,3},{5,4},{6,5},{7,6},{8,7},{9,8},{10,9},{11,1... | collective-permute-start | bytes 344072 | tf_op jit(solution)/shard_map/ppermute | solution.py:39

commit v3 on v2

v3 whole, which is shorter than its diff:
```python
import jax
import jax.numpy as jnp
from jax import lax
from jax.experimental import pallas as pl
from jax.experimental.pallas import tpu as pltpu
from jax.sharding import PartitionSpec as P

GX = 32
GY = 16
AXES = ("gx", "gy")
BF = jnp.bfloat16
F32 = jnp.float32
VMEM = pl.BlockSpec(memory_space=pltpu.VMEM)
HBM = pl.BlockSpec(memory_space=pltpu.HBM)
ROOM = 2048
SMALL = 4 * 1024 * 1024


def in_hbm(value):
    return pltpu.with_memory_space_constraint(value, pltpu.HBM)


def in_vmem(value):
    return pltpu.VMEM(value.shape, value.dtype)


def rank(x, y):
    return x * GY + y


NEAR = [(rank(x, y), rank(x ^ 1, y)) for x in range(GX) for y in range(GY)]
FAR = [
    (rank(x, y), rank(((x + 1) ^ 1) - 1, y)) for x in range(1, GX - 1) for y in range(GY)
]
UP = [(rank(x, y), rank(x, y + 1)) for x in range(GX) for y in range(GY - 1)]
DOWN = [(j, i) for i, j in UP]


def send(value, pairs):
    return lax.ppermute(value, AXES, pairs)


def fill_x(edge, coarse, skip, first):
    for half in range(2):
        edge[half * 64 : half * 64 + 64] = coarse[:, half * 128 : half * 128 + 128]
    edge[128:384] = skip[pl.ds(first, 2)].reshape(256, 128)


def fetch(sources, targets, sems):
    copies = [
        pltpu.make_async_copy(source, target, sems.at[i])
        for i, (source, target) in enumerate(zip(sources, targets))
    ]
    for copy in copies:
        copy.start()
    return copies


def is_first():
    return (lax.axis_index("gx") // 2) % 4 == 0


def fields_kernel(*refs):
    (coarse_in, skip_in), sources, (coarse, skip, far) = refs[:2], refs[2:8], refs[8:11]
    targets, sems, weight_sems = refs[11:17], refs[17], refs[18]
    odd = lax.axis_index("gx") % 2
    for copy in fetch((coarse_in, skip_in), (coarse, skip), sems):
        copy.wait()
    fill_x(far, coarse, skip, 2 * odd)

    @pl.when(is_first())
    def _():
        for copy in fetch(sources, targets, weight_sems):
            copy.wait()


def fields(coarse, skip, weights):
    return pl.pallas_call(
        fields_kernel,
        out_shape=[in_vmem(coarse), in_vmem(skip), pltpu.VMEM((384, 128), BF)]
        + [in_vmem(w) for w in weights],
        in_specs=[HBM] * 8,
        out_specs=[VMEM] * 9,
        scratch_shapes=[pltpu.SemaphoreType.DMA((2,)), pltpu.SemaphoreType.DMA((6,))],
        compiler_params=pltpu.CompilerParams(vmem_limit_bytes=SMALL),
    )(in_hbm(coarse), in_hbm(skip), *[in_hbm(w) for w in weights])


def stage_kernel(*refs):
    sources, coarse, skip = refs[:6], refs[12], refs[13]
    targets, near, sems = refs[14:20], refs[20], refs[22]
    odd = lax.axis_index("gx") % 2
    fill_x(near, coarse, skip, 2 - 2 * odd)

    @pl.when(jnp.logical_not(is_first()))
    def _():
        for copy in fetch(sources, targets, sems):
            copy.wait()


def stage(weights, held, coarse, skip):
    return pl.pallas_call(
        stage_kernel,
        out_shape=[in_vmem(w) for w in weights] + [pltpu.VMEM((384, 128), BF), pltpu.VMEM((ROOM, 128), BF)],
        in_specs=[HBM] * 6 + [VMEM] * 8,
        out_specs=[VMEM] * 8,
        input_output_aliases={6 + i: i for i in range(6)},
        scratch_shapes=[pltpu.SemaphoreType.DMA((6,))],
        compiler_params=pltpu.CompilerParams(vmem_limit_bytes=SMALL),
        cost_estimate=pl.CostEstimate(flops=0, bytes_accessed=14_000_000, transcendentals=0),
    )(*[in_hbm(w) for w in weights], *held, coarse, skip)


def pack_y_kernel(coarse, skip, far, near, room, up, down):
    for out, first in ((down, 0), (up, 1)):
        for half in range(2):
            for x in range(2):
                row = half * 96 + x * 16
                at = x * 32 + first * 16
                out[row : row + 16] = coarse[at : at + 16, half * 128 : half * 128 + 128]
                for s, source in ((1, near), (2, far)):
                    row = half * 96 + s * 32 + x * 16
                    at = half * 64 + x * 32 + first * 16
                    out[row : row + 16] = source[at : at + 16]
        out[192:320] = skip[:, first * 6 : first * 6 + 2].reshape(128, 128)
        for s, source in ((0, near), (1, far)):
            for x in range(2):
                row = 320 + s * 64 + x * 32
                at = 128 + x * 128 + first * 96
                out[row : row + 32] = source[at : at + 32]


def pack_y(coarse, skip, far, near, room):
    edge = jax.ShapeDtypeStruct((448, 128), BF)
    return pl.pallas_call(
        pack_y_kernel,
        out_shape=(edge, edge),
        in_specs=[VMEM] * 5,
        out_specs=(VMEM, VMEM),
        compiler_params=pltpu.CompilerParams(vmem_limit_bytes=SMALL),
    )(coarse, skip, far, near, room)


TAPS = (((1, 1), (3, 0)), ((0, 2), (2, 1)))


def later(value):
    return jnp.concatenate([jnp.zeros_like(value[:, :1]), value[:, :-1]], 1)


def earlier(value):
    return jnp.concatenate([value[:, 1:], jnp.zeros_like(value[:, :1])], 1)


def upsample(cells, uw, bias, mixed, px, py, spans):
    lhs = []
    rhs = []
    for kx, ix in TAPS[px]:
        for ky, iy in TAPS[py]:
            parts = [cells[ix : ix + 4, iy + start : iy + stop] for start, stop in spans]
            block = jnp.concatenate(parts, 1) if len(parts) > 1 else parts[0]
            lhs.append(block.reshape(96, 256).astype(BF))
            at = kx * 16 + ky * 4
            rhs.append(jnp.concatenate([uw[at + kz] for kz in range(4)], 1))
    terms = jnp.dot(
        jnp.concatenate(lhs, 1), jnp.concatenate(rhs, 0), preferred_element_type=F32
    ).reshape(12, 8, 512)
    mixed[:, pl.ds(0, 8, 2), :] = terms[:, :, 128:256] + later(terms[:, :, 384:512]) + bias
    mixed[:, pl.ds(1, 8, 2), :] = terms[:, :, 256:384] + earlier(terms[:, :, 0:128]) + bias


def first_conv(joined, kernel, bias, x, count, spans):
    lhs = []
    rows = sum(stop - start for start, stop in spans)
    for dx in range(3):
        for dy in range(3):
            parts = [
                joined[x + dx : x + dx + count, start + dy : stop + dy] for start, stop in spans
            ]
            block = jnp.concatenate(parts, 1) if len(parts) > 1 else parts[0]
            lhs.append(block.reshape(count * rows * 16, 256))
    terms = jnp.dot(jnp.concatenate(lhs, 1), kernel, preferred_element_type=F32)
    terms = terms.reshape(count * rows, 16, 384)
    value = (
        terms[:, :, 128:256] + later(terms[:, :, 0:128]) + earlier(terms[:, :, 256:384]) + bias
    )
    return jnp.maximum(value, 0.0).astype(BF).reshape(count, rows, 16, 128)


def x_places():
    odd = lax.axis_index("gx") % 2
    return 4 - 4 * odd, 4 * odd, 6 - 6 * odd, 6 * odd


def inner_kernel(
    coarse, skip, near, far, uw, ub, fw, fb, upsampled, middle, cells, joined, mixed
):
    gx = lax.axis_index("gx")
    near_c, far_c, near_f, far_f = x_places()
    for half in range(2):
        lanes = slice(half * 128, half * 128 + 128)
        cells[2:4, 2:6, :, lanes] = coarse[:, lanes].astype(F32).reshape(2, 4, 8, 128)
        for at, source in ((near_c, near), (far_c, far)):
            cells[pl.ds(at, 2), 2:6, :, lanes] = (
                source[half * 64 : half * 64 + 64].astype(F32).reshape(2, 4, 8, 128)
            )
    joined[2:6, :, :, 128:256] = skip[:, 1:7]
    for at, source in ((near_f, near), (far_f, far)):
        for x in range(2):
            row = 128 + x * 128
            joined[at + x, :, :, 128:256] = source[row + 16 : row + 112].reshape(6, 16, 128)
    for px in range(2):
        for py in range(2):
            upsample(cells, uw, ub[...], mixed, px, py, ((2 - py, 5 - py),))
            for a in range(4):
                for b in range(3):
                    joined[2 * a + px, 2 * b + 1 - py, :, 0:128] = mixed[a * 3 + b].astype(BF)

    @pl.when(gx == 0)
    def _():
        joined[0:2, :, :, 0:128] = jnp.zeros((2, 6, 16, 128), BF)

    @pl.when(gx == GX - 1)
    def _():
        joined[6:8, :, :, 0:128] = jnp.zeros((2, 6, 16, 128), BF)

    upsampled[...] = joined[:, :, :, 0:128]
    kernel = jnp.concatenate([fw[:, dz].reshape(2304, 128) for dz in range(3)], 1)
    middle[...] = first_conv(joined, kernel, fb[...], 0, 6, ((0, 4),))


def inner(coarse, skip, near, far, uw, ub, fw, fb):
    return pl.pallas_call(
        inner_kernel,
        out_shape=(pltpu.VMEM((8, 6, 16, 128), BF), pltpu.VMEM((6, 4, 16, 128), BF)),
        in_specs=[VMEM] * 8,
        out_specs=(VMEM, VMEM),
        scratch_shapes=[
            pltpu.VMEM((6, 8, 8, 256), F32),
            pltpu.VMEM((8, 6, 16, 256), BF),
            pltpu.VMEM((12, 16, 128), F32),
        ],
        compiler_params=pltpu.CompilerParams(vmem_limit_bytes=16 * 1024 * 1024),
        cost_estimate=pl.CostEstimate(flops=2_500_000_000, bytes_accessed=0, transcendentals=0),
    )(coarse, skip, near, far, uw, ub, fw, fb)


def outer_kernel(
    coarse, skip, near, far, low, high, upsampled, middle, uw, ub, fw, fb, sw, sb, out,
    cells, joined, hidden, mixed,
):
    gx = lax.axis_index("gx")
    gy = lax.axis_index("gy")
    near_c, far_c, near_f, far_f = x_places()
    for half in range(2):
        lanes = slice(half * 128, half * 128 + 128)
        cells[2:4, 2:6, :, lanes] = coarse[:, lanes].astype(F32).reshape(2, 4, 8, 128)
        for at, source in ((near_c, near), (far_c, far)):
            cells[pl.ds(at, 2), 2:6, :, lanes] = (
                source[half * 64 : half * 64 + 64].astype(F32).reshape(2, 4, 8, 128)
            )
        for at, source in ((0, low), (6, high)):
            for s, x in ((0, 2), (1, near_c), (2, far_c)):
                row = half * 96 + s * 32
                cells[pl.ds(x, 2), at : at + 2, :, lanes] = (
                    source[row : row + 32].astype(F32).reshape(2, 2, 8, 128)
                )
    joined[2:6, 2:10, :, 128:256] = skip[...]
    joined[pl.ds(near_f, 2), 2:10, :, 128:256] = near[128:384].reshape(2, 8, 16, 128)
    joined[pl.ds(far_f, 2), 2:10, :, 128:256] = far[128:384].reshape(2, 8, 16, 128)
    for at, source in ((0, low), (10, high)):
        joined[2:6, at : at + 2, :, 128:256] = source[192:320].reshape(4, 2, 16, 128)
        joined[pl.ds(near_f, 2), at : at + 2, :, 128:256] = source[320:384].reshape(2, 2, 16, 128)
        joined[pl.ds(far_f, 2), at : at + 2, :, 128:256] = source[384:448].reshape(2, 2, 16, 128)
    joined[:, 3:9, :, 0:128] = upsampled[...]
    hidden[:, 3:7] = middle[...]
    for px in range(2):
        for py in range(2):
            spans = ((0, 2 - py), (5 - py, 6))
            upsample(cells, uw, ub[...], mixed, px, py, spans)
            places = [b for start, stop in spans for b in range(start, stop)]
            for a in range(4):
                for i, b in enumerate(places):
                    joined[2 * a + px, 2 * b + py, :, 0:128] = mixed[a * 3 + i].astype(BF)

    @pl.when(gx == 0)
    def _():
        joined[0:2, :, :, 0:128] = jnp.zeros((2, 12, 16, 128), BF)

    @pl.when(gx == GX - 1)
    def _():
        joined[6:8, :, :, 0:128] = jnp.zeros((2, 12, 16, 128), BF)

    @pl.when(gy == 0)
    def _():
        joined[:, 0:2, :, 0:128] = jnp.zeros((8, 2, 16, 128), BF)

    @pl.when(gy == GY - 1)
    def _():
        joined[:, 10:12, :, 0:128] = jnp.zeros((8, 2, 16, 128), BF)

    kernel = jnp.concatenate([fw[:, dz].reshape(2304, 128) for dz in range(3)], 1)
    for x in (0, 3):
        value = first_conv(joined, kernel, fb[...], x, 3, ((0, 3), (7, 10)))
        hidden[x : x + 3, 0:3] = value[:, 0:3]
        hidden[x : x + 3, 7:10] = value[:, 3:6]

    @pl.when(gx == 0)
    def _():
        hidden[0:1] = jnp.zeros((1, 10, 16, 128), BF)

    @pl.when(gx == GX - 1)
    def _():
        hidden[5:6] = jnp.zeros((1, 10, 16, 128), BF)

    @pl.when(gy == 0)
    def _():
        hidden[:, 0:1] = jnp.zeros((6, 1, 16, 128), BF)

    @pl.when(gy == GY - 1)
    def _():
        hidden[:, 9:10] = jnp.zeros((6, 1, 16, 128), BF)

    kernel = jnp.concatenate([sw[:, dz].reshape(1152, 128) for dz in range(3)], 1)
    for x in range(0, 4, 2):
        lhs = [
            hidden[x + dx : x + dx + 2, dy : dy + 8].reshape(256, 128)
            for dx in range(3)
            for dy in range(3)
        ]
        terms = jnp.dot(jnp.concatenate(lhs, 1), kernel, preferred_element_type=F32)
        terms = terms.reshape(16, 16, 384)
        value = (
            terms[:, :, 128:256]
            + later(terms[:, :, 0:128])
            + earlier(terms[:, :, 256:384])
            + sb[...]
        )
        out[x : x + 2] = value.astype(BF).reshape(2, 8, 16, 128)


def outer(coarse, skip, near, far, low, high, upsampled, middle, *weights):
    return pl.pallas_call(
        outer_kernel,
        out_shape=jax.ShapeDtypeStruct((4, 8, 16, 128), BF),
        in_specs=[VMEM] * 14,
        out_specs=VMEM,
        scratch_shapes=[
            pltpu.VMEM((6, 8, 8, 256), F32),
            pltpu.VMEM((8, 12, 16, 256), BF),
            pltpu.VMEM((6, 10, 16, 128), BF),
            pltpu.VMEM((12, 16, 128), F32),
        ],
        compiler_params=pltpu.CompilerParams(vmem_limit_bytes=24 * 1024 * 1024),
        cost_estimate=pl.CostEstimate(flops=3_000_000_000, bytes_accessed=0, transcendentals=0),
    )(coarse, skip, near, far, low, high, upsampled, middle, *weights)


def per_device(coarse, skip, up_weight, up_bias, first_weight, first_bias, second_weight, second_bias):
    weights = (
        up_weight.reshape(64, 256, 128),
        up_bias.reshape(1, 128),
        first_weight.reshape(9, 3, 256, 128),
        first_bias.reshape(1, 128),
        second_weight.reshape(9, 3, 128, 128),
        second_bias.reshape(1, 128),
    )
    coarse, skip, far, *held = fields(coarse.reshape(64, 256), skip, weights)
    far = send(far, FAR)
    *weights, near, room = stage(weights, held, coarse, skip)
    near = send(near, NEAR)
    up, down = pack_y(coarse, skip, far, near, room)
    low = send(up, UP)
    high = send(down, DOWN)
    upsampled, middle = inner(coarse, skip, near, far, *weights[:4])
    return outer(coarse, skip, near, far, low, high, upsampled, middle, *weights)


def solution(mesh):
    return jax.shard_map(
        per_device,
        mesh=mesh,
        in_specs=(P("gx", "gy"), P("gx", "gy"), P(), P(), P(), P(), P(), P()),
        out_specs=P("gx", "gy"),
        check_vma=False,
    )
```

time: 36.5 us -> 33.7 us (0.923)
  starting transfers between devices: 20.2 us -> 17.2 us
  Pallas kernels: 9.07 us -> 10 us
  waiting for transfers between devices: 6.93 us -> 6.15 us
    pallas_call x3 -> x4, Pallas kernels: 6.03 us -> 9.94 us  [the longest x1 3.98 us: fields(): pl.pallas_call(fields_kernel, out_shape=[in_vmem(coarse), in_vmem(skip),...]
    ppermute x4, starting transfers between devices: 20.2 us -> 17.2 us  [send(): return lax.ppermute(value, AXES, pairs)]
    pallas_call x1, Pallas kernels: 3.04 us -> 0.09 us  [stage(): pl.pallas_call(stage_kernel, out_shape=[in_vmem(w) for w in weights] + [p...]
    ppermute x4, waiting for transfers between devices: 6.93 us -> 6.15 us  [send(): return lax.ppermute(value, AXES, pairs)]
  transfers between devices with their start and end apart: 4 -> 4, of which waited for: 4 -> 2; matrix products, arithmetic and copies ran while one was open for 0% -> 0% of each run, Pallas kernels for 8% -> 6%
where the time goes in v3:
time: 33.7 us; the launch traced here: 33.5 us
  starting transfers between devices  17.2 us (51%)
  Pallas kernels  10 us (30%)
  waiting for transfers between devices  6.15 us (18%)
    ppermute x4, starting transfers between devices, send(): return lax.ppermute(value, AXES, pairs)  17.2 us
    ppermute x4, waiting for transfers between devices, send(): return lax.ppermute(value, AXES, pairs)  6.15 us
    pallas_call x1, Pallas kernels, fields(): pl.pallas_call(fields_kernel, out_shape=[in_vmem(coarse), in_vmem(skip),...  3.98 us
    pallas_call x1, Pallas kernels, outer(): pl.pallas_call(outer_kernel, out_shape=jax.ShapeDtypeStruct((4, 8, 16, 12...  3.97 us
    pallas_call x1, Pallas kernels, inner(): pl.pallas_call(inner_kernel, out_shape=(pltpu.VMEM((8, 6, 16, 128), BF),...  1.98 us
  transfers between devices with their start and end apart: 4, of which 2 were waited for; matrix products, arithmetic and copies ran while one was open for 0% of the time, Pallas kernels for 6%

profile of v3, /device:TPU:30, one launch (start us, length us, event | category | flops | bytes accessed | tf_op | source)
XLA Modules:
  0.0 33.5 jit_solution(618161571448338425)
XLA Ops:
  0.0 4.0 %shard_map.82 = (bf16[64,256]{1,0:T(8,128)(2,1)S(1)}, bf16[4,8,16,128]{3,2,1,0:T(8,128)(2,1)S(1)}, bf16[384,128]{1,0:T(8,128)(2,1)S(1)}, bf16[64,256,128]{2,1,0:...) custom-call(bf16[64,256]{1,0:T(8,128)(2,1)} %bitcast.13, ...), custom_call_target="tpu_custom_call" | custom-call | tf_op jit(solution)/shard_map/pallas_call | solution.py:78
  4.0 9.5 %collective-permute-start.1 = (bf16[384,128]{1,0:T(8,128)(2,1)S(1)}, bf16[384,128]{1,0:T(8,128)(2,1)S(1)}, u32[]{:S(2)}, u32[]{:S(2)}) collective-permute-start(bf16[384,128]{1,0:T(8,128)(2,1)S(1)} %get-tuple-element.35), channel_id=1, source_target_pairs={{16,32},{17,33},{18,34},{19,35},{20,36},{21,37},{22,38},{23,39},{2... | collective-permute-start | bytes 294920 | tf_op jit(solution)/shard_map/ppermute | solution.py:40
  13.5 0.1 shard_map.83
  13.6 1.9 %collective-permute-start = (bf16[384,128]{1,0:T(8,128)(2,1)S(1)}, bf16[384,128]{1,0:T(8,128)(2,1)S(1)}, u32[]{:S(2)}, u32[]{:S(2)}) collective-permute-start(bf16[384,128]{1,0:T(8,128)(2,1)S(1)} %get-tuple-element.34), channel_id=1, source_target_pairs={{0,16},{1,17},{2,18},{3,19},{4,20},{5,21},{6,22},{7,23},{8,24},{9,... | collective-permute-start | bytes 294920 | tf_op jit(solution)/shard_map/ppermute | solution.py:40
  15.5 3.3 %collective-permute-done.1.far = bf16[384,128]{1,0:T(8,128)(2,1)S(1)} collective-permute-done((bf16[384,128]{1,0:T(8,128)(2,1)S(1)}, bf16[384,128]{1,0:T(8,128)(2,1)S(1)}, u32[]{:S(2)}, u32[]{:S(2)}) %collective-permute-start.1) | collective-permute-done | bytes 98336 | tf_op jit(solution)/shard_map/ppermute | solution.py:40
  18.8 0.0 collective-permute-done.near
  18.8 1.9 %collective-permute-start.2 = (bf16[448,128]{1,0:T(8,128)(2,1)S(1)}, bf16[448,128]{1,0:T(8,128)(2,1)S(1)}, u32[]{:S(2)}, u32[]{:S(2)}) collective-permute-start(bf16[448,128]{1,0:T(8,128)(2,1)S(1)} %get-tuple-element.37), channel_id=1, source_target_pairs={{0,1},{1,2},{2,3},{3,4},{4,5},{5,6},{6,7},{7,8},{8,9},{9,10},{10,1... | collective-permute-start | bytes 344072 | tf_op jit(solution)/shard_map/ppermute | solution.py:40
  20.7 3.9 %collective-permute-start.3 = (bf16[448,128]{1,0:T(8,128)(2,1)S(1)}, bf16[448,128]{1,0:T(8,128)(2,1)S(1)}, u32[]{:S(2)}, u32[]{:S(2)}) collective-permute-start(bf16[448,128]{1,0:T(8,128)(2,1)S(1)} %get-tuple-element.38), channel_id=1, source_target_pairs={{1,0},{2,1},{3,2},{4,3},{5,4},{6,5},{7,6},{8,7},{9,8},{10,9},{11,1... | collective-permute-start | bytes 344072 | tf_op jit(solution)/shard_map/ppermute | solution.py:40
  24.7 2.0 %shard_map.85 = (bf16[8,6,16,128]{3,2,1,0:T(8,128)(2,1)S(1)}, bf16[6,4,16,128]{3,2,1,0:T(8,128)(2,1)S(1)}) custom-call(bf16[64,256]{1,0:T(8,128)(2,1)S(1)} %get-tuple-element.26.refs_12_.coarse, bf16[4,8,16,128]{3,2,1,0:T(8,128)(2,1)S(1)} %get-tuple-element.27.refs_13_.skip, bf16[384,128]{1,0:T(8,128)(2,1)S(1)} %collective-permute-done.near, ...), custom_call_target="tpu_custom_call" | custom-call | flops 2500000000 | tf_op jit(solution)/shard_map/pallas_call | solution.py:233
  26.6 0.0 collective-permute-done.2.low
  26.6 2.9 %collective-permute-done.3.high = bf16[448,128]{1,0:T(8,128)(2,1)S(1)} collective-permute-done((bf16[448,128]{1,0:T(8,128)(2,1)S(1)}, bf16[448,128]{1,0:T(8,128)(2,1)S(1)}, u32[]{:S(2)}, u32[]{:S(2)}) %collective-permute-start.3) | collective-permute-done | bytes 114720 | tf_op jit(solution)/shard_map/ppermute | solution.py:40
  29.5 4.0 %shard_map.86 = bf16[4,8,16,128]{3,2,1,0:T(8,128)(2,1)} custom-call(bf16[64,256]{1,0:T(8,128)(2,1)S(1)} %get-tuple-element.26.refs_12_.coarse, bf16[4,8,16,128]{3,2,1,0:T(8,128)(2,1)S(1)} %get-tuple-element.27.refs_13_.skip, bf16[384,128]{1,0:T(8,128)(2,1)S(1)} %collective-permute-done.near, bf16[384,128]{1,0:T(8,128)(2,1)S(1)} %collective-permute-done.1.far, ...), custom_call_target="tpu_custom_call" | custom-call | flops 3000000000 | tf_op jit(solution)/shard_map/pallas_call | solution.py:343
  (1 shorter events, 0.0 us)
Async XLA Ops:
  4.0 14.8 %collective-permute-start.1 = (bf16[384,128]{1,0:T(8,128)(2,1)S(1)}, bf16[384,128]{1,0:T(8,128)(2,1)S(1)}, u32[]{:S(2)}, u32[]{:S(2)}) collective-permute-start(bf16[384,128]{1,0:T(8,128)(2,1)S(1)} %get-tuple-element.35), channel_id=1, source_target_pairs={{16,32},{17,33},{18,34},{19,35},{20,36},{21,37},{22,38},{23,39},{2... | collective-permute-start | bytes 294920 | tf_op jit(solution)/shard_map/ppermute | solution.py:40
  13.6 5.2 %collective-permute-start = (bf16[384,128]{1,0:T(8,128)(2,1)S(1)}, bf16[384,128]{1,0:T(8,128)(2,1)S(1)}, u32[]{:S(2)}, u32[]{:S(2)}) collective-permute-start(bf16[384,128]{1,0:T(8,128)(2,1)S(1)} %get-tuple-element.34), channel_id=1, source_target_pairs={{0,16},{1,17},{2,18},{3,19},{4,20},{5,21},{6,22},{7,23},{8,24},{9,... | collective-permute-start | bytes 294920 | tf_op jit(solution)/shard_map/ppermute | solution.py:40
  18.8 7.8 %collective-permute-start.2 = (bf16[448,128]{1,0:T(8,128)(2,1)S(1)}, bf16[448,128]{1,0:T(8,128)(2,1)S(1)}, u32[]{:S(2)}, u32[]{:S(2)}) collective-permute-start(bf16[448,128]{1,0:T(8,128)(2,1)S(1)} %get-tuple-element.37), channel_id=1, source_target_pairs={{0,1},{1,2},{2,3},{3,4},{4,5},{5,6},{6,7},{7,8},{8,9},{9,10},{10,1... | collective-permute-start | bytes 344072 | tf_op jit(solution)/shard_map/ppermute | solution.py:40
  20.7 8.8 %collective-permute-start.3 = (bf16[448,128]{1,0:T(8,128)(2,1)S(1)}, bf16[448,128]{1,0:T(8,128)(2,1)S(1)}, u32[]{:S(2)}, u32[]{:S(2)}) collective-permute-start(bf16[448,128]{1,0:T(8,128)(2,1)S(1)} %get-tuple-element.38), channel_id=1, source_target_pairs={{1,0},{2,1},{3,2},{4,3},{5,4},{6,5},{7,6},{8,7},{9,8},{10,9},{11,1... | collective-permute-start | bytes 344072 | tf_op jit(solution)/shard_map/ppermute | solution.py:40

commit v4 on v3

--- a/solution.py
+++ b/solution.py
@@ -169,22 +169,60 @@
     mixed[:, pl.ds(1, 8, 2), :] = terms[:, :, 256:384] + earlier(terms[:, :, 0:128]) + bias
 
 
-def first_conv(joined, kernel, bias, x, count, spans):
+def taps_side_by_side(weight, depth):
+    return jnp.concatenate([weight[:, dz].reshape(9 * depth, 128) for dz in range(3)], 1)
+
+
+def conv(field, kernel, bias, x, count, spans):
+    depth = field.shape[3]
     lhs = []
     rows = sum(stop - start for start, stop in spans)
     for dx in range(3):
         for dy in range(3):
-            parts = [
-                joined[x + dx : x + dx + count, start + dy : stop + dy] for start, stop in spans
-            ]
+            parts = [field[x + dx : x + dx + count, start + dy : stop + dy] for start, stop in spans]
             block = jnp.concatenate(parts, 1) if len(parts) > 1 else parts[0]
-            lhs.append(block.reshape(count * rows * 16, 256))
+            lhs.append(block.reshape(count * rows * 16, depth))
     terms = jnp.dot(jnp.concatenate(lhs, 1), kernel, preferred_element_type=F32)
     terms = terms.reshape(count * rows, 16, 384)
     value = (
         terms[:, :, 128:256] + later(terms[:, :, 0:128]) + earlier(terms[:, :, 256:384]) + bias
     )
-    return jnp.maximum(value, 0.0).astype(BF).reshape(count, rows, 16, 128)
+    return value.reshape(count, rows, 16, 128)
+
+
+def row_terms(field, kernel, x, count, spans):
+    lhs = []
+    rows = sum(stop - start for start, stop in spans)
+    for dx in range(3):
+        parts = [field[x + dx : x + dx + count, start:stop] for start, stop in spans]
+        block = jnp.concatenate(parts, 1) if len(parts) > 1 else parts[0]
+        lhs.append(block.reshape(count * rows * 16, 256))
+    terms = jnp.dot(jnp.concatenate(lhs, 1), kernel, preferred_element_type=F32)
+    return terms.reshape(count, rows, 16, 384)
+
+
+def row_kernels(weight):
+    return [
+        jnp.concatenate(
+            [
+                jnp.concatenate([weight[3 * dx + dy, dz] for dz in range(3)], 1)
+                for dx in range(3)
+            ],
+            0,
+        )
+        for dy in range(3)
+    ]
+
+
+def along_z(terms):
+    count, rows = terms.shape[:2]
+    terms = terms.reshape(count * rows, 16, 384)
+    value = terms[:, :, 128:256] + later(terms[:, :, 0:128]) + earlier(terms[:, :, 256:384])
+    return value.reshape(count, rows, 16, 128)
+
+
+def rectified(value):
+    return jnp.maximum(value, 0.0).astype(BF)
 
 
 def x_places():
@@ -193,7 +231,7 @@
 
 
 def inner_kernel(
-    coarse, skip, near, far, uw, ub, fw, fb, upsampled, middle, cells, joined, mixed
+    coarse, skip, near, far, uw, ub, fw, fb, sw, sb, upsampled, middle, core, begun, cells, joined, mixed
 ):
     gx = lax.axis_index("gx")
     near_c, far_c, near_f, far_f = x_places()
@@ -225,16 +263,46 @@
         joined[6:8, :, :, 0:128] = jnp.zeros((2, 6, 16, 128), BF)
 
     upsampled[...] = joined[:, :, :, 0:128]
-    kernel = jnp.concatenate([fw[:, dz].reshape(2304, 128) for dz in range(3)], 1)
-    middle[...] = first_conv(joined, kernel, fb[...], 0, 6, ((0, 4),))
-
-
-def inner(coarse, skip, near, far, uw, ub, fw, fb):
+    kernel = taps_side_by_side(fw, 256)
+    middle[...] = rectified(conv(joined, kernel, fb[...], 0, 6, ((0, 4),)))
+
+    @pl.when(gx == 0)
+    def _():
+        middle[0:1] = jnp.zeros((1, 4, 16, 128), BF)
+
+    @pl.when(gx == GX - 1)
+    def _():
+        middle[5:6] = jnp.zeros((1, 4, 16, 128), BF)
+
+    kernels = row_kernels(fw)
+    below = row_terms(joined, kernels[0], 0, 6, ((4, 6),))
+    level = row_terms(joined, kernels[1], 0, 6, ((0, 1), (5, 6)))
+    above = row_terms(joined, kernels[2], 0, 6, ((0, 2),))
+    begun[...] = along_z(
+        jnp.concatenate(
+            [
+                above[:, 0:1],
+                above[:, 1:2] + level[:, 0:1],
+                below[:, 0:1] + level[:, 1:2],
+                below[:, 1:2],
+            ],
+            1,
+        )
+    )
+    core[...] = conv(middle, taps_side_by_side(sw, 128), sb[...], 0, 4, ((0, 2),)).astype(BF)
+
+
+def inner(coarse, skip, near, far, *weights):
     return pl.pallas_call(
         inner_kernel,
-        out_shape=(pltpu.VMEM((8, 6, 16, 128), BF), pltpu.VMEM((6, 4, 16, 128), BF)),
-        in_specs=[VMEM] * 8,
-        out_specs=(VMEM, VMEM),
+        out_shape=(
+            pltpu.VMEM((8, 6, 16, 128), BF),
+            pltpu.VMEM((6, 4, 16, 128), BF),
+            pltpu.VMEM((4, 2, 16, 128), BF),
+            pltpu.VMEM((6, 4, 16, 128), F32),
+        ),
+        in_specs=[VMEM] * 10,
+        out_specs=[VMEM] * 4,
         scratch_shapes=[
             pltpu.VMEM((6, 8, 8, 256), F32),
             pltpu.VMEM((8, 6, 16, 256), BF),
@@ -242,12 +310,12 @@
         ],
         compiler_params=pltpu.CompilerParams(vmem_limit_bytes=16 * 1024 * 1024),
         cost_estimate=pl.CostEstimate(flops=2_500_000_000, bytes_accessed=0, transcendentals=0),
-    )(coarse, skip, near, far, uw, ub, fw, fb)
+    )(coarse, skip, near, far, *weights)
 
 
 def outer_kernel(
-    coarse, skip, near, far, low, high, upsampled, middle, uw, ub, fw, fb, sw, sb, out,
-    cells, joined, hidden, mixed,
+    coarse, skip, near, far, low, high, upsampled, middle, core, begun, uw, ub, fw, fb, sw, sb, out,
+    cells, joined, hidden, mixed, result, sems,
 ):
     gx = lax.axis_index("gx")
     gy = lax.axis_index("gy")
@@ -274,6 +342,7 @@
         joined[pl.ds(far_f, 2), at : at + 2, :, 128:256] = source[384:448].reshape(2, 2, 16, 128)
     joined[:, 3:9, :, 0:128] = upsampled[...]
     hidden[:, 3:7] = middle[...]
+    result[:, 3:5] = core[...]
     for px in range(2):
         for py in range(2):
             spans = ((0, 2 - py), (5 - py, 6))
@@ -299,11 +368,29 @@
     def _():
         joined[:, 10:12, :, 0:128] = jnp.zeros((8, 2, 16, 128), BF)
 
-    kernel = jnp.concatenate([fw[:, dz].reshape(2304, 128) for dz in range(3)], 1)
+    kernels = row_kernels(fw)
     for x in (0, 3):
-        value = first_conv(joined, kernel, fb[...], x, 3, ((0, 3), (7, 10)))
-        hidden[x : x + 3, 0:3] = value[:, 0:3]
-        hidden[x : x + 3, 7:10] = value[:, 3:6]
+        below = row_terms(joined, kernels[0], x, 3, ((0, 3), (9, 10)))
+        level = row_terms(joined, kernels[1], x, 3, ((1, 3), (9, 11)))
+        above = row_terms(joined, kernels[2], x, 3, ((2, 3), (9, 12)))
+        value = along_z(
+            jnp.concatenate(
+                [
+                    below[:, 0:1] + level[:, 0:1] + above[:, 0:1],
+                    below[:, 1:2] + level[:, 1:2],
+                    below[:, 2:3],
+                    above[:, 1:2],
+                    level[:, 2:3] + above[:, 2:3],
+                    below[:, 3:4] + level[:, 3:4] + above[:, 3:4],
+                ],
+                1,
+            )
+        )
+        started = begun[x : x + 3]
+        hidden[x : x + 3, 0:1] = rectified(value[:, 0:1] + fb[...])
+        hidden[x : x + 3, 1:3] = rectified(value[:, 1:3] + started[:, 0:2] + fb[...])
+        hidden[x : x + 3, 7:9] = rectified(value[:, 3:5] + started[:, 2:4] + fb[...])
+        hidden[x : x + 3, 9:10] = rectified(value[:, 5:6] + fb[...])
 
     @pl.when(gx == 0)
     def _():
@@ -321,39 +408,39 @@
     def _():
         hidden[:, 9:10] = jnp.zeros((6, 1, 16, 128), BF)
 
-    kernel = jnp.concatenate([sw[:, dz].reshape(1152, 128) for dz in range(3)], 1)
-    for x in range(0, 4, 2):
-        lhs = [
-            hidden[x + dx : x + dx + 2, dy : dy + 8].reshape(256, 128)
-            for dx in range(3)
-            for dy in range(3)
-        ]
-        terms = jnp.dot(jnp.concatenate(lhs, 1), kernel, preferred_element_type=F32)
-        terms = terms.reshape(16, 16, 384)
-        value = (
-            terms[:, :, 128:256]
-            + later(terms[:, :, 0:128])
-            + earlier(terms[:, :, 256:384])
-            + sb[...]
+    kernel = taps_side_by_side(sw, 128)
+    copies = []
+    for half in range(2):
+        x = 2 * half
+        value = conv(hidden, kernel, sb[...], x, 2, ((0, 3), (5, 8))).astype(BF)
+        result[x : x + 2, 0:3] = value[:, 0:3]
+        result[x : x + 2, 5:8] = value[:, 3:6]
+        copy = pltpu.make_async_copy(
+            result.at[x : x + 2], out.at[x : x + 2], sems.at[half]
         )
-        out[x : x + 2] = value.astype(BF).reshape(2, 8, 16, 128)
-
-
-def outer(coarse, skip, near, far, low, high, upsampled, middle, *weights):
+        copy.start()
+        copies.append(copy)
+    for copy in copies:
+        copy.wait()
+
+
+def outer(coarse, skip, near, far, low, high, upsampled, middle, core, begun, *weights):
     return pl.pallas_call(
         outer_kernel,
-        out_shape=jax.ShapeDtypeStruct((4, 8, 16, 128), BF),
-        in_specs=[VMEM] * 14,
-        out_specs=VMEM,
+        out_shape=pltpu.HBM((4, 8, 16, 128), BF),
+        in_specs=[VMEM] * 16,
+        out_specs=HBM,
         scratch_shapes=[
             pltpu.VMEM((6, 8, 8, 256), F32),
             pltpu.VMEM((8, 12, 16, 256), BF),
             pltpu.VMEM((6, 10, 16, 128), BF),
             pltpu.VMEM((12, 16, 128), F32),
+            pltpu.VMEM((4, 8, 16, 128), BF),
+            pltpu.SemaphoreType.DMA((2,)),
         ],
         compiler_params=pltpu.CompilerParams(vmem_limit_bytes=24 * 1024 * 1024),
         cost_estimate=pl.CostEstimate(flops=3_000_000_000, bytes_accessed=0, transcendentals=0),
-    )(coarse, skip, near, far, low, high, upsampled, middle, *weights)
+    )(coarse, skip, near, far, low, high, upsampled, middle, core, begun, *weights)
 
 
 def per_device(coarse, skip, up_weight, up_bias, first_weight, first_bias, second_weight, second_bias):
@@ -372,8 +459,8 @@
     up, down = pack_y(coarse, skip, far, near, room)
     low = send(up, UP)
     high = send(down, DOWN)
-    upsampled, middle = inner(coarse, skip, near, far, *weights[:4])
-    return outer(coarse, skip, near, far, low, high, upsampled, middle, *weights)
+    upsampled, middle, core, begun = inner(coarse, skip, near, far, *weights)
+    return outer(coarse, skip, near, far, low, high, upsampled, middle, core, begun, *weights)
 
 
 def solution(mesh):

time: 33.7 us -> 33 us (0.979)
  waiting for transfers between devices: 6.15 us -> 5.35 us
    pallas_call x1, Pallas kernels: 1.98 us -> 2.78 us  [inner(): pl.pallas_call(inner_kernel, out_shape=(pltpu.VMEM((8, 6, 16, 128), BF),...]
    ppermute x4, waiting for transfers between devices: 6.15 us -> 5.35 us  [send(): return lax.ppermute(value, AXES, pairs)]
    pallas_call x1, Pallas kernels: 3.97 us -> 3.32 us  [outer(): pl.pallas_call(outer_kernel, out_shape=pltpu.HBM((4, 8, 16, 128), BF), in...]
  transfers between devices with their start and end apart: 4 -> 4, of which waited for: 2 -> 2; matrix products, arithmetic and copies ran while one was open for 0% -> 0% of each run, Pallas kernels for 6% -> 9%
where the time goes in v4:
time: 33 us; the launch traced here: 32.8 us
  starting transfers between devices  17.2 us (52%)
  Pallas kernels  10.2 us (31%)
  waiting for transfers between devices  5.35 us (16%)
    ppermute x4, starting transfers between devices, send(): return lax.ppermute(value, AXES, pairs)  17.2 us
    ppermute x4, waiting for transfers between devices, send(): return lax.ppermute(value, AXES, pairs)  5.35 us
    pallas_call x1, Pallas kernels, fields(): pl.pallas_call(fields_kernel, out_shape=[in_vmem(coarse), in_vmem(skip),...  3.98 us
    pallas_call x1, Pallas kernels, outer(): pl.pallas_call(outer_kernel, out_shape=pltpu.HBM((4, 8, 16, 128), BF), in...  3.32 us
    pallas_call x1, Pallas kernels, inner(): pl.pallas_call(inner_kernel, out_shape=(pltpu.VMEM((8, 6, 16, 128), BF),...  2.78 us
  transfers between devices with their start and end apart: 4, of which 2 were waited for; matrix products, arithmetic and copies ran while one was open for 0% of the time, Pallas kernels for 9%

profile of v4, /device:TPU:30, one launch (start us, length us, event | category | flops | bytes accessed | tf_op | source)
XLA Modules:
  0.0 32.8 jit_solution(4958654590516344862)
XLA Ops:
  0.0 4.0 %shard_map.82 = (bf16[64,256]{1,0:T(8,128)(2,1)S(1)}, bf16[4,8,16,128]{3,2,1,0:T(8,128)(2,1)S(1)}, bf16[384,128]{1,0:T(8,128)(2,1)S(1)}, bf16[64,256,128]{2,1,0:...) custom-call(bf16[64,256]{1,0:T(8,128)(2,1)} %bitcast.13, ...), custom_call_target="tpu_custom_call" | custom-call | tf_op jit(solution)/shard_map/pallas_call | solution.py:78
  4.0 9.5 %collective-permute-start.1 = (bf16[384,128]{1,0:T(8,128)(2,1)S(1)}, bf16[384,128]{1,0:T(8,128)(2,1)S(1)}, u32[]{:S(2)}, u32[]{:S(2)}) collective-permute-start(bf16[384,128]{1,0:T(8,128)(2,1)S(1)} %get-tuple-element.37), channel_id=1, source_target_pairs={{16,32},{17,33},{18,34},{19,35},{20,36},{21,37},{22,38},{23,39},{2... | collective-permute-start | bytes 294920 | tf_op jit(solution)/shard_map/ppermute | solution.py:40
  13.5 0.1 shard_map.83
  13.6 1.9 %collective-permute-start = (bf16[384,128]{1,0:T(8,128)(2,1)S(1)}, bf16[384,128]{1,0:T(8,128)(2,1)S(1)}, u32[]{:S(2)}, u32[]{:S(2)}) collective-permute-start(bf16[384,128]{1,0:T(8,128)(2,1)S(1)} %get-tuple-element.36), channel_id=1, source_target_pairs={{0,16},{1,17},{2,18},{3,19},{4,20},{5,21},{6,22},{7,23},{8,24},{9,... | collective-permute-start | bytes 294920 | tf_op jit(solution)/shard_map/ppermute | solution.py:40
  15.5 3.3 %collective-permute-done.1.far = bf16[384,128]{1,0:T(8,128)(2,1)S(1)} collective-permute-done((bf16[384,128]{1,0:T(8,128)(2,1)S(1)}, bf16[384,128]{1,0:T(8,128)(2,1)S(1)}, u32[]{:S(2)}, u32[]{:S(2)}) %collective-permute-start.1) | collective-permute-done | bytes 98336 | tf_op jit(solution)/shard_map/ppermute | solution.py:40
  18.8 0.0 collective-permute-done.near
  18.8 1.9 %collective-permute-start.2 = (bf16[448,128]{1,0:T(8,128)(2,1)S(1)}, bf16[448,128]{1,0:T(8,128)(2,1)S(1)}, u32[]{:S(2)}, u32[]{:S(2)}) collective-permute-start(bf16[448,128]{1,0:T(8,128)(2,1)S(1)} %get-tuple-element.39), channel_id=1, source_target_pairs={{0,1},{1,2},{2,3},{3,4},{4,5},{5,6},{6,7},{7,8},{8,9},{9,10},{10,1... | collective-permute-start | bytes 344072 | tf_op jit(solution)/shard_map/ppermute | solution.py:40
  20.7 3.9 %collective-permute-start.3 = (bf16[448,128]{1,0:T(8,128)(2,1)S(1)}, bf16[448,128]{1,0:T(8,128)(2,1)S(1)}, u32[]{:S(2)}, u32[]{:S(2)}) collective-permute-start(bf16[448,128]{1,0:T(8,128)(2,1)S(1)} %get-tuple-element.40), channel_id=1, source_target_pairs={{1,0},{2,1},{3,2},{4,3},{5,4},{6,5},{7,6},{8,7},{9,8},{10,9},{11,1... | collective-permute-start | bytes 344072 | tf_op jit(solution)/shard_map/ppermute | solution.py:40
  24.7 2.8 %shard_map.85 = (bf16[8,6,16,128]{3,2,1,0:T(8,128)(2,1)S(1)}, bf16[6,4,16,128]{3,2,1,0:T(8,128)(2,1)S(1)}, bf16[4,2,16,128]{3,2,1,0:T(8,128)(2,1)S(1)}, f32[6,4,16,128]{3,2,1,0:T(8,128)S(1)}) custom-call(bf16[64,256]{1,0:T(8,128)(2,1)S(1)} %get-tuple-element.28.refs_12_.coarse, bf16[4,8,16,128]{3,2,1,0:T(8,128)(2,1)S(1)} %get-tuple-element.29.refs_13_.skip, ...), custom_call_target="tpu_custom_call" | custom-call | flops 2500000000 | tf_op jit(solution)/shard_map/pallas_call | solution.py:296
  27.4 0.0 collective-permute-done.2.low
  27.5 2.1 %collective-permute-done.3.high = bf16[448,128]{1,0:T(8,128)(2,1)S(1)} collective-permute-done((bf16[448,128]{1,0:T(8,128)(2,1)S(1)}, bf16[448,128]{1,0:T(8,128)(2,1)S(1)}, u32[]{:S(2)}, u32[]{:S(2)}) %collective-permute-start.3) | collective-permute-done | bytes 114720 | tf_op jit(solution)/shard_map/ppermute | solution.py:40
  29.5 3.3 %shard_map.86 = bf16[4,8,16,128]{3,2,1,0:T(8,128)(2,1)} custom-call(bf16[64,256]{1,0:T(8,128)(2,1)S(1)} %get-tuple-element.28.refs_12_.coarse, bf16[4,8,16,128]{3,2,1,0:T(8,128)(2,1)S(1)} %get-tuple-element.29.refs_13_.skip, bf16[384,128]{1,0:T(8,128)(2,1)S(1)} %collective-permute-done.near, bf16[384,128]{1,0:T(8,128)(2,1)S(1)} %collective-permute-done.1.far, ...), custom_call_target="tpu_custom_call" | custom-call | flops 3000000000 | tf_op jit(solution)/shard_map/pallas_call | solution.py:428
  (1 shorter events, 0.0 us)
Async XLA Ops:
  4.0 14.8 %collective-permute-start.1 = (bf16[384,128]{1,0:T(8,128)(2,1)S(1)}, bf16[384,128]{1,0:T(8,128)(2,1)S(1)}, u32[]{:S(2)}, u32[]{:S(2)}) collective-permute-start(bf16[384,128]{1,0:T(8,128)(2,1)S(1)} %get-tuple-element.37), channel_id=1, source_target_pairs={{16,32},{17,33},{18,34},{19,35},{20,36},{21,37},{22,38},{23,39},{2... | collective-permute-start | bytes 294920 | tf_op jit(solution)/shard_map/ppermute | solution.py:40
  13.6 5.2 %collective-permute-start = (bf16[384,128]{1,0:T(8,128)(2,1)S(1)}, bf16[384,128]{1,0:T(8,128)(2,1)S(1)}, u32[]{:S(2)}, u32[]{:S(2)}) collective-permute-start(bf16[384,128]{1,0:T(8,128)(2,1)S(1)} %get-tuple-element.36), channel_id=1, source_target_pairs={{0,16},{1,17},{2,18},{3,19},{4,20},{5,21},{6,22},{7,23},{8,24},{9,... | collective-permute-start | bytes 294920 | tf_op jit(solution)/shard_map/ppermute | solution.py:40
  18.8 8.6 %collective-permute-start.2 = (bf16[448,128]{1,0:T(8,128)(2,1)S(1)}, bf16[448,128]{1,0:T(8,128)(2,1)S(1)}, u32[]{:S(2)}, u32[]{:S(2)}) collective-permute-start(bf16[448,128]{1,0:T(8,128)(2,1)S(1)} %get-tuple-element.39), channel_id=1, source_target_pairs={{0,1},{1,2},{2,3},{3,4},{4,5},{5,6},{6,7},{7,8},{8,9},{9,10},{10,1... | collective-permute-start | bytes 344072 | tf_op jit(solution)/shard_map/ppermute | solution.py:40
  20.7 8.8 %collective-permute-start.3 = (bf16[448,128]{1,0:T(8,128)(2,1)S(1)}, bf16[448,128]{1,0:T(8,128)(2,1)S(1)}, u32[]{:S(2)}, u32[]{:S(2)}) collective-permute-start(bf16[448,128]{1,0:T(8,128)(2,1)S(1)} %get-tuple-element.40), channel_id=1, source_target_pairs={{1,0},{2,1},{3,2},{4,3},{5,4},{6,5},{7,6},{8,7},{9,8},{10,9},{11,1... | collective-permute-start | bytes 344072 | tf_op jit(solution)/shard_map/ppermute | solution.py:40

commit v5 on v4

--- a/solution.py
+++ b/solution.py
@@ -196,7 +196,7 @@
     for dx in range(3):
         parts = [field[x + dx : x + dx + count, start:stop] for start, stop in spans]
         block = jnp.concatenate(parts, 1) if len(parts) > 1 else parts[0]
-        lhs.append(block.reshape(count * rows * 16, 256))
+        lhs.append(block.reshape(count * rows * 16, field.shape[3]))
     terms = jnp.dot(jnp.concatenate(lhs, 1), kernel, preferred_element_type=F32)
     return terms.reshape(count, rows, 16, 384)
 
@@ -231,7 +231,7 @@
 
 
 def inner_kernel(
-    coarse, skip, near, far, uw, ub, fw, fb, sw, sb, upsampled, middle, core, begun, cells, joined, mixed
+    coarse, skip, near, far, uw, ub, fw, fb, sw, sb, upsampled, middle, core, begun, begun_out, cells, joined, mixed
 ):
     gx = lax.axis_index("gx")
     near_c, far_c, near_f, far_f = x_places()
@@ -289,6 +289,21 @@
             1,
         )
     )
+    kernels = row_kernels(sw)
+    below = row_terms(middle, kernels[0], 0, 4, ((2, 4),))
+    level = row_terms(middle, kernels[1], 0, 4, ((0, 1), (3, 4)))
+    above = row_terms(middle, kernels[2], 0, 4, ((0, 2),))
+    begun_out[...] = along_z(
+        jnp.concatenate(
+            [
+                above[:, 0:1],
+                above[:, 1:2] + level[:, 0:1],
+                below[:, 0:1] + level[:, 1:2],
+                below[:, 1:2],
+            ],
+            1,
+        )
+    )
     core[...] = conv(middle, taps_side_by_side(sw, 128), sb[...], 0, 4, ((0, 2),)).astype(BF)
 
 
@@ -300,9 +315,10 @@
             pltpu.VMEM((6, 4, 16, 128), BF),
             pltpu.VMEM((4, 2, 16, 128), BF),
             pltpu.VMEM((6, 4, 16, 128), F32),
+            pltpu.VMEM((4, 4, 16, 128), F32),
         ),
         in_specs=[VMEM] * 10,
-        out_specs=[VMEM] * 4,
+        out_specs=[VMEM] * 5,
         scratch_shapes=[
             pltpu.VMEM((6, 8, 8, 256), F32),
             pltpu.VMEM((8, 6, 16, 256), BF),
@@ -314,7 +330,7 @@
 
 
 def outer_kernel(
-    coarse, skip, near, far, low, high, upsampled, middle, core, begun, uw, ub, fw, fb, sw, sb, out,
+    coarse, skip, near, far, low, high, upsampled, middle, core, begun, begun_out, uw, ub, fw, fb, sw, sb, out,
     cells, joined, hidden, mixed, result, sems,
 ):
     gx = lax.axis_index("gx")
@@ -408,13 +424,31 @@
     def _():
         hidden[:, 9:10] = jnp.zeros((6, 1, 16, 128), BF)
 
-    kernel = taps_side_by_side(sw, 128)
+    kernels = row_kernels(sw)
     copies = []
     for half in range(2):
         x = 2 * half
-        value = conv(hidden, kernel, sb[...], x, 2, ((0, 3), (5, 8))).astype(BF)
-        result[x : x + 2, 0:3] = value[:, 0:3]
-        result[x : x + 2, 5:8] = value[:, 3:6]
+        below = row_terms(hidden, kernels[0], x, 2, ((0, 3), (7, 8)))
+        level = row_terms(hidden, kernels[1], x, 2, ((1, 3), (7, 9)))
+        above = row_terms(hidden, kernels[2], x, 2, ((2, 3), (7, 10)))
+        value = along_z(
+            jnp.concatenate(
+                [
+                    below[:, 0:1] + level[:, 0:1] + above[:, 0:1],
+                    below[:, 1:2] + level[:, 1:2],
+                    below[:, 2:3],
+                    above[:, 1:2],
+                    level[:, 2:3] + above[:, 2:3],
+                    below[:, 3:4] + level[:, 3:4] + above[:, 3:4],
+                ],
+                1,
+            )
+        )
+        started = begun_out[x : x + 2]
+        result[x : x + 2, 0:1] = (value[:, 0:1] + sb[...]).astype(BF)
+        result[x : x + 2, 1:3] = (value[:, 1:3] + started[:, 0:2] + sb[...]).astype(BF)
+        result[x : x + 2, 5:7] = (value[:, 3:5] + started[:, 2:4] + sb[...]).astype(BF)
+        result[x : x + 2, 7:8] = (value[:, 5:6] + sb[...]).astype(BF)
         copy = pltpu.make_async_copy(
             result.at[x : x + 2], out.at[x : x + 2], sems.at[half]
         )
@@ -424,11 +458,11 @@
         copy.wait()
 
 
-def outer(coarse, skip, near, far, low, high, upsampled, middle, core, begun, *weights):
+def outer(coarse, skip, near, far, low, high, upsampled, middle, core, begun, begun_out, *weights):
     return pl.pallas_call(
         outer_kernel,
         out_shape=pltpu.HBM((4, 8, 16, 128), BF),
-        in_specs=[VMEM] * 16,
+        in_specs=[VMEM] * 17,
         out_specs=HBM,
         scratch_shapes=[
             pltpu.VMEM((6, 8, 8, 256), F32),
@@ -440,7 +474,7 @@
         ],
         compiler_params=pltpu.CompilerParams(vmem_limit_bytes=24 * 1024 * 1024),
         cost_estimate=pl.CostEstimate(flops=3_000_000_000, bytes_accessed=0, transcendentals=0),
-    )(coarse, skip, near, far, low, high, upsampled, middle, core, begun, *weights)
+    )(coarse, skip, near, far, low, high, upsampled, middle, core, begun, begun_out, *weights)
 
 
 def per_device(coarse, skip, up_weight, up_bias, first_weight, first_bias, second_weight, second_bias):
@@ -459,8 +493,8 @@
     up, down = pack_y(coarse, skip, far, near, room)
     low = send(up, UP)
     high = send(down, DOWN)
-    upsampled, middle, core, begun = inner(coarse, skip, near, far, *weights)
-    return outer(coarse, skip, near, far, low, high, upsampled, middle, core, begun, *weights)
+    upsampled, middle, core, begun, begun_out = inner(coarse, skip, near, far, *weights)
+    return outer(coarse, skip, near, far, low, high, upsampled, middle, core, begun, begun_out, *weights)
 
 
 def solution(mesh):

time: 33 us -> 32.9 us (level)
  no operation moved by 1% of the time
where the time goes in v5:
time: 32.9 us; the launch traced here: 32.7 us
  starting transfers between devices  17.2 us (52%)
  Pallas kernels  10.3 us (31%)
  waiting for transfers between devices  5.16 us (16%)
    ppermute x4, starting transfers between devices, send(): return lax.ppermute(value, AXES, pairs)  17.2 us
    ppermute x4, waiting for transfers between devices, send(): return lax.ppermute(value, AXES, pairs)  5.16 us
    pallas_call x1, Pallas kernels, fields(): pl.pallas_call(fields_kernel, out_shape=[in_vmem(coarse), in_vmem(skip),...  3.98 us
    pallas_call x1, Pallas kernels, outer(): pl.pallas_call(outer_kernel, out_shape=pltpu.HBM((4, 8, 16, 128), BF), in...  3.2 us
    pallas_call x1, Pallas kernels, inner(): pl.pallas_call(inner_kernel, out_shape=(pltpu.VMEM((8, 6, 16, 128), BF),...  2.96 us
  transfers between devices with their start and end apart: 4, of which 2 were waited for; matrix products, arithmetic and copies ran while one was open for 0% of the time, Pallas kernels for 9%

profile of v5, /device:TPU:30, one launch (start us, length us, event | category | flops | bytes accessed | tf_op | source)
XLA Modules:
  0.0 32.7 jit_solution(7548803981986650605)
XLA Ops:
  0.0 4.0 %shard_map.82 = (bf16[64,256]{1,0:T(8,128)(2,1)S(1)}, bf16[4,8,16,128]{3,2,1,0:T(8,128)(2,1)S(1)}, bf16[384,128]{1,0:T(8,128)(2,1)S(1)}, bf16[64,256,128]{2,1,0:...) custom-call(bf16[64,256]{1,0:T(8,128)(2,1)} %bitcast.13, ...), custom_call_target="tpu_custom_call" | custom-call | tf_op jit(solution)/shard_map/pallas_call | solution.py:78
  4.0 9.5 %collective-permute-start.1 = (bf16[384,128]{1,0:T(8,128)(2,1)S(1)}, bf16[384,128]{1,0:T(8,128)(2,1)S(1)}, u32[]{:S(2)}, u32[]{:S(2)}) collective-permute-start(bf16[384,128]{1,0:T(8,128)(2,1)S(1)} %get-tuple-element.38), channel_id=1, source_target_pairs={{16,32},{17,33},{18,34},{19,35},{20,36},{21,37},{22,38},{23,39},{2... | collective-permute-start | bytes 294920 | tf_op jit(solution)/shard_map/ppermute | solution.py:40
  13.5 0.1 shard_map.83
  13.6 1.9 %collective-permute-start = (bf16[384,128]{1,0:T(8,128)(2,1)S(1)}, bf16[384,128]{1,0:T(8,128)(2,1)S(1)}, u32[]{:S(2)}, u32[]{:S(2)}) collective-permute-start(bf16[384,128]{1,0:T(8,128)(2,1)S(1)} %get-tuple-element.37), channel_id=1, source_target_pairs={{0,16},{1,17},{2,18},{3,19},{4,20},{5,21},{6,22},{7,23},{8,24},{9,... | collective-permute-start | bytes 294920 | tf_op jit(solution)/shard_map/ppermute | solution.py:40
  15.5 3.3 %collective-permute-done.1.far = bf16[384,128]{1,0:T(8,128)(2,1)S(1)} collective-permute-done((bf16[384,128]{1,0:T(8,128)(2,1)S(1)}, bf16[384,128]{1,0:T(8,128)(2,1)S(1)}, u32[]{:S(2)}, u32[]{:S(2)}) %collective-permute-start.1) | collective-permute-done | bytes 98336 | tf_op jit(solution)/shard_map/ppermute | solution.py:40
  18.8 0.0 collective-permute-done.near
  18.8 1.9 %collective-permute-start.2 = (bf16[448,128]{1,0:T(8,128)(2,1)S(1)}, bf16[448,128]{1,0:T(8,128)(2,1)S(1)}, u32[]{:S(2)}, u32[]{:S(2)}) collective-permute-start(bf16[448,128]{1,0:T(8,128)(2,1)S(1)} %get-tuple-element.40), channel_id=1, source_target_pairs={{0,1},{1,2},{2,3},{3,4},{4,5},{5,6},{6,7},{7,8},{8,9},{9,10},{10,1... | collective-permute-start | bytes 344072 | tf_op jit(solution)/shard_map/ppermute | solution.py:40
  20.7 3.9 %collective-permute-start.3 = (bf16[448,128]{1,0:T(8,128)(2,1)S(1)}, bf16[448,128]{1,0:T(8,128)(2,1)S(1)}, u32[]{:S(2)}, u32[]{:S(2)}) collective-permute-start(bf16[448,128]{1,0:T(8,128)(2,1)S(1)} %get-tuple-element.41), channel_id=1, source_target_pairs={{1,0},{2,1},{3,2},{4,3},{5,4},{6,5},{7,6},{8,7},{9,8},{10,9},{11,1... | collective-permute-start | bytes 344072 | tf_op jit(solution)/shard_map/ppermute | solution.py:40
  24.7 3.0 %shard_map.85 = (bf16[8,6,16,128]{3,2,1,0:T(8,128)(2,1)S(1)}, bf16[6,4,16,128]{3,2,1,0:T(8,128)(2,1)S(1)}, bf16[4,2,16,128]{3,2,1,0:T(8,128)(2,1)S(1)}, f32[6,4,...) custom-call(bf16[64,256]{1,0:T(8,128)(2,1)S(1)} %get-tuple-element.29.refs_12_.coarse, ...), custom_call_target="tpu_custom_call" | custom-call | flops 2500000000 | tf_op jit(solution)/shard_map/pallas_call | solution.py:311
  27.6 0.0 collective-permute-done.2.low
  27.6 1.9 %collective-permute-done.3.high = bf16[448,128]{1,0:T(8,128)(2,1)S(1)} collective-permute-done((bf16[448,128]{1,0:T(8,128)(2,1)S(1)}, bf16[448,128]{1,0:T(8,128)(2,1)S(1)}, u32[]{:S(2)}, u32[]{:S(2)}) %collective-permute-start.3) | collective-permute-done | bytes 114720 | tf_op jit(solution)/shard_map/ppermute | solution.py:40
  29.5 3.2 %shard_map.86 = bf16[4,8,16,128]{3,2,1,0:T(8,128)(2,1)} custom-call(bf16[64,256]{1,0:T(8,128)(2,1)S(1)} %get-tuple-element.29.refs_12_.coarse, bf16[4,8,16,128]{3,2,1,0:T(8,128)(2,1)S(1)} %get-tuple-element.30.refs_13_.skip, bf16[384,128]{1,0:T(8,128)(2,1)S(1)} %collective-permute-done.near, bf16[384,128]{1,0:T(8,128)(2,1)S(1)} %collective-permute-done.1.far, ...), custom_call_target="tpu_custom_call" | custom-call | flops 3000000000 | tf_op jit(solution)/shard_map/pallas_call | solution.py:462
  (1 shorter events, 0.0 us)
Async XLA Ops:
  4.0 14.8 %collective-permute-start.1 = (bf16[384,128]{1,0:T(8,128)(2,1)S(1)}, bf16[384,128]{1,0:T(8,128)(2,1)S(1)}, u32[]{:S(2)}, u32[]{:S(2)}) collective-permute-start(bf16[384,128]{1,0:T(8,128)(2,1)S(1)} %get-tuple-element.38), channel_id=1, source_target_pairs={{16,32},{17,33},{18,34},{19,35},{20,36},{21,37},{22,38},{23,39},{2... | collective-permute-start | bytes 294920 | tf_op jit(solution)/shard_map/ppermute | solution.py:40
  13.6 5.2 %collective-permute-start = (bf16[384,128]{1,0:T(8,128)(2,1)S(1)}, bf16[384,128]{1,0:T(8,128)(2,1)S(1)}, u32[]{:S(2)}, u32[]{:S(2)}) collective-permute-start(bf16[384,128]{1,0:T(8,128)(2,1)S(1)} %get-tuple-element.37), channel_id=1, source_target_pairs={{0,16},{1,17},{2,18},{3,19},{4,20},{5,21},{6,22},{7,23},{8,24},{9,... | collective-permute-start | bytes 294920 | tf_op jit(solution)/shard_map/ppermute | solution.py:40
  18.8 8.8 %collective-permute-start.2 = (bf16[448,128]{1,0:T(8,128)(2,1)S(1)}, bf16[448,128]{1,0:T(8,128)(2,1)S(1)}, u32[]{:S(2)}, u32[]{:S(2)}) collective-permute-start(bf16[448,128]{1,0:T(8,128)(2,1)S(1)} %get-tuple-element.40), channel_id=1, source_target_pairs={{0,1},{1,2},{2,3},{3,4},{4,5},{5,6},{6,7},{7,8},{8,9},{9,10},{10,1... | collective-permute-start | bytes 344072 | tf_op jit(solution)/shard_map/ppermute | solution.py:40
  20.7 8.8 %collective-permute-start.3 = (bf16[448,128]{1,0:T(8,128)(2,1)S(1)}, bf16[448,128]{1,0:T(8,128)(2,1)S(1)}, u32[]{:S(2)}, u32[]{:S(2)}) collective-permute-start(bf16[448,128]{1,0:T(8,128)(2,1)S(1)} %get-tuple-element.41), channel_id=1, source_target_pairs={{1,0},{2,1},{3,2},{4,3},{5,4},{6,5},{7,6},{8,7},{9,8},{10,9},{11,1... | collective-permute-start | bytes 344072 | tf_op jit(solution)/shard_map/ppermute | solution.py:40
